TPU v7x, 32 devices: a whole 2x2x4 slice. The times are simulated.
32 devices in a mesh: depth: 4 (over x, core), tile: 8 (over z, y).
Axes of the slice: x: 2, y: 2, z: 4, core: 2. Of those that a mesh axis runs over, the one named last changes fastest.
Arguments:
- incident: float32 [2, 3, 256, 512], P(None, None, 'tile'), may hold values from -6 to 6
- delta: float32 [3, 8, 256, 512], P(None, 'depth', 'tile'), may hold values from 0 to 1
- beta: float32 [3, 8, 256, 512], P(None, 'depth', 'tile'), may hold values from 0 to 0.5
- view_order: int32 [3], replicated, may hold values from 0 to 2, each once
Outputs:
- slab_waves: float32 [2, 3, 4, 256, 512], P(None, None, 'depth', 'tile')
Inputs may be any that keep to these rules, and one draw needn't show every extreme that they name: `view_order`: each view appears once.
All inputs are finite; a program needn't handle non-finite values.
Results may differ from a plain program's by a relative error of at most 0.0001.
Values sent between devices are 32-bit elements; how exact they have to be, the bound alone decides.
A program may use at most 64 MiB of HBM per device.

v0:
```python
import jax
import jax.numpy as jnp
from jax import lax
from jax.sharding import PartitionSpec as P

HALF = 32
COL_BLOCK = 256


def padded_2(block, sides, width):
    for axis, dim in sides:
        count = lax.axis_size(axis)
        forward = [(i, i + 1) for i in range(count - 1)]
        backward = [(target, source) for source, target in forward]
        low = lax.ppermute(
            lax.slice_in_dim(block, block.shape[dim] - width, None, axis=dim), axis, forward
        )
        high = lax.ppermute(lax.slice_in_dim(block, 0, width, axis=dim), axis, backward)
        block = jnp.concatenate([low, block, high], axis=dim)
    return block


def passed_along(value, axis, steps):
    count = lax.axis_size(axis)
    first, last = (max(0, -steps), min(count, count - steps))
    return lax.ppermute(value, axis, [(source, source + steps) for source in range(first, last)])


def tap_values(offset, half):
    grid = jnp.arange(-half, half + 1).astype(jnp.float32)
    window = 0.75 + 0.25 * jnp.cos(jnp.pi * grid / (half + 1))
    angle = jnp.pi * grid * grid / (6.25 * half)
    norm = jnp.sqrt(jnp.sum(window * jnp.cos(angle)) ** 2 + jnp.sum(window * jnp.sin(angle)) ** 2)
    place = offset.astype(jnp.float32)
    inside = jnp.abs(offset) <= half
    shape_win = 0.75 + 0.25 * jnp.cos(jnp.pi * place / (half + 1))
    turn = jnp.pi * place * place / (6.25 * half)
    real_part = jnp.where(inside, shape_win * jnp.cos(turn), 0.0) / norm
    imag_part = jnp.where(inside, shape_win * jnp.sin(turn), 0.0) / norm
    return (real_part, imag_part)


def column_matrix(block, half):
    source = lax.broadcasted_iota(jnp.int32, (block + 2 * half, block), 0)
    target = lax.broadcasted_iota(jnp.int32, (block + 2 * half, block), 1)
    real_part, imag_part = tap_values(source - half - target, half)
    upper = jnp.concatenate([real_part, imag_part], axis=1)
    lower = jnp.concatenate([-imag_part, real_part], axis=1)
    return jnp.concatenate([upper, lower], axis=0)


def row_matrix(rows, half):
    target = lax.broadcasted_iota(jnp.int32, (rows, rows + 2 * half), 0)
    source = lax.broadcasted_iota(jnp.int32, (rows, rows + 2 * half), 1)
    real_part, imag_part = tap_values(source - half - target, half)
    upper = jnp.concatenate([real_part, -imag_part], axis=1)
    lower = jnp.concatenate([imag_part, real_part], axis=1)
    return jnp.concatenate([upper, lower], axis=0)


def blur_columns(field, cmat, block, half):
    width = field.shape[-1]
    padded = jnp.pad(field, ((0, 0), (0, 0), (0, 0), (half, half)))
    windows = jnp.stack(
        [padded[..., b * block : b * block + block + 2 * half] for b in range(width // block)],
        axis=3,
    )
    joined = jnp.concatenate([windows[0], windows[1]], axis=-1)
    result = jnp.dot(
        joined, cmat, precision=lax.Precision.HIGHEST, preferred_element_type=jnp.float32
    )
    lead = field.shape[1:3]
    real_part = result[..., :block].reshape(lead + (width,))
    imag_part = result[..., block:].reshape(lead + (width,))
    return jnp.stack([real_part, imag_part])


def blur_rows(wide, rmat):
    stacked = jnp.concatenate([wide[0], wide[1]], axis=1)
    result = jnp.einsum(
        "oi,vic->voc",
        rmat,
        stacked,
        precision=lax.Precision.HIGHEST,
        preferred_element_type=jnp.float32,
    )
    rows = rmat.shape[0] // 2
    return jnp.stack([result[:, :rows], result[:, rows:]])


def with_rims(field, half):
    return padded_2(field, (("tile", 2),), half)


def propagate(field, slab_delta, slab_beta, cmat, rmat, block, half):
    for piece in range(slab_delta.shape[1]):
        amp = jnp.exp(-slab_beta[:, piece])
        phase = -jnp.pi * slab_delta[:, piece]
        trans_re = amp * jnp.cos(phase)
        trans_im = amp * jnp.sin(phase)
        field = jnp.stack(
            [field[0] * trans_re - field[1] * trans_im, field[0] * trans_im + field[1] * trans_re]
        )
        wide = blur_rows(with_rims(field, half), rmat)
        field = blur_columns(wide, cmat, block, half)
    return field


def per_device(incident, delta, beta, view_order):
    half = HALF
    block = COL_BLOCK
    views = incident.shape[1]
    rows = incident.shape[2]
    cmat = column_matrix(block, half)
    rmat = row_matrix(rows, half)
    section = lax.axis_index("depth")
    sections = lax.axis_size("depth")
    slab_out = jnp.zeros((2, views, 1) + incident.shape[2:], jnp.float32)
    slots = lax.broadcasted_iota(jnp.int32, (1, views, 1, 1, 1), 1)
    previous = incident[:, :1]
    for step in range(views + sections - 1):
        slot = step - section
        clipped = jnp.clip(slot, 0, views - 1)
        view = view_order[clipped]
        start = lax.dynamic_slice_in_dim(incident, view, 1, 1)
        if step == 0:
            state = start
        else:
            arrived = passed_along(previous, "depth", 1)
            state = jnp.where(section == 0, start, arrived)
        slab_delta = lax.dynamic_slice_in_dim(delta, view, 1, 0)
        slab_beta = lax.dynamic_slice_in_dim(beta, view, 1, 0)
        result = propagate(state, slab_delta, slab_beta, cmat, rmat, block, half)
        active = (slots == slot) & (slot >= 0) & (slot < views)
        slab_out = jnp.where(active, result[:, :, None], slab_out)
        previous = result
    return slab_out


def solution(mesh):
    return jax.shard_map(
        per_device,
        mesh=mesh,
        in_specs=(
            P(None, None, "tile", None),
            P(None, "depth", "tile", None),
            P(None, "depth", "tile", None),
            P(),
        ),
        out_specs=P(None, None, "depth", "tile", None),
        check_vma=False,
    )
```

profile of v0, /device:TPU:0, one launch (start us, length us, event | category | flops | bytes accessed | tf_op | source)
XLA Modules:
  0.0 187.7 jit_solution(8441885078049537151)
XLA Ops:
  0.0 1.5 fusion.150
  3.4 1.2 multiply_subtract_fusion.11
  4.6 1.3 collective-permute-start.1
  5.9 5.5 %collective-permute-start = (f32[2,1,32,512]{3,2,1,0:T(8,128)S(1)}, f32[2,1,32,512]{3,2,1,0:T(8,128)S(1)}, u32[]{:S(2)}, u32[]{:S(2)}) collective-permute-start(f32[2,1,32,512]{3,2,1,0:T(8,128)S(1)} %pad_maximum_fusion.12), channel_id=1, source_target_pairs={{0,1},{1,2},{2,3},{3,4},{4,5},{5,6},{6,7},{8,9},{9,10},{10,11},{11... | collective-permute-start | bytes 393224 | tf_op jit(solution)/shard_map/ppermute | solution.py:15
  15.5 2.5 %select_divide_fusion = (f32[320,256]{1,0:T(8,128)S(1)}, f32[320,256]{1,0:T(8,128)S(1)}, f32[320,256]{1,0:T(8,128)S(1)}) fusion(f32[]{:T(128)S(6)} %sqrt.4, s32[320]{0:T(512)S(1)} %iota_add_fusion), kind=kLoop, calls=%fused_computation.76 | loop fusion | flops 1392640 | bytes 984324 | tf_op jit(solution)/shard_map/div | solution.py:39
  21.1 1.3 collective-permute-start.3
  22.4 5.5 %collective-permute-start.2 = (f32[2,1,32,512]{3,2,1,0:T(8,128)S(1)}, f32[2,1,32,512]{3,2,1,0:T(8,128)S(1)}, u32[]{:S(2)}, u32[]{:S(2)}) collective-permute-start(f32[2,1,32,512]{3,2,1,0:T(8,128)S(1)} %pad_maximum_fusion.13), channel_id=1, source_target_pairs={{0,1},{1,2},{2,3},{3,4},{4,5},{5,6},{6,7},{8,9},{9,10},{10,11},{11... | collective-permute-start | bytes 393224 | tf_op jit(solution)/shard_map/ppermute | solution.py:15
  27.9 1.0 collective-permute-done.3
  28.9 2.9 %collective-permute-done.2 = f32[2,1,32,512]{3,2,1,0:T(8,128)S(1)} collective-permute-done((f32[2,1,32,512]{3,2,1,0:T(8,128)S(1)}, f32[2,1,32,512]{3,2,1,0:T(8,128)S(1)}, u32[]{:S(2)}, u32[]{:S(2)}) %collective-permute-start.2) | collective-permute-done | bytes 131104 | tf_op jit(solution)/shard_map/ppermute | solution.py:15
  32.5 0.9 convolution_bitcast_fusion.22
  33.7 1.7 collective-permute-start.4
  37.6 1.3 collective-permute-start.6
  38.9 5.0 %collective-permute-start.5 = (f32[2,1,32,512]{3,2,1,0:T(8,128)S(1)}, f32[2,1,32,512]{3,2,1,0:T(8,128)S(1)}, u32[]{:S(2)}, u32[]{:S(2)}) collective-permute-start(f32[2,1,32,512]{3,2,1,0:T(8,128)S(1)} %pad_maximum_fusion.14), channel_id=1, source_target_pairs={{0,1},{1,2},{2,3},{3,4},{4,5},{5,6},{6,7},{8,9},{9,10},{10,11},{11... | collective-permute-start | bytes 393224 | tf_op jit(solution)/shard_map/ppermute | solution.py:15
  44.0 1.2 collective-permute-done.6
  45.2 4.3 %collective-permute-done.5 = f32[2,1,32,512]{3,2,1,0:T(8,128)S(1)} collective-permute-done((f32[2,1,32,512]{3,2,1,0:T(8,128)S(1)}, f32[2,1,32,512]{3,2,1,0:T(8,128)S(1)}, u32[]{:S(2)}, u32[]{:S(2)}) %collective-permute-start.5) | collective-permute-done | bytes 131104 | tf_op jit(solution)/shard_map/ppermute | solution.py:15
  50.2 0.9 convolution_bitcast_fusion.21
  51.7 1.3 collective-permute-start.8
  53.0 5.0 %collective-permute-start.7 = (f32[2,1,32,512]{3,2,1,0:T(8,128)S(1)}, f32[2,1,32,512]{3,2,1,0:T(8,128)S(1)}, u32[]{:S(2)}, u32[]{:S(2)}) collective-permute-start(f32[2,1,32,512]{3,2,1,0:T(8,128)S(1)} %pad_maximum_fusion.15), channel_id=1, source_target_pairs={{0,1},{1,2},{2,3},{3,4},{4,5},{5,6},{6,7},{8,9},{9,10},{10,11},{11... | collective-permute-start | bytes 393224 | tf_op jit(solution)/shard_map/ppermute | solution.py:15
  58.0 1.8 collective-permute-done.8
  59.8 3.0 %collective-permute-done.7 = f32[2,1,32,512]{3,2,1,0:T(8,128)S(1)} collective-permute-done((f32[2,1,32,512]{3,2,1,0:T(8,128)S(1)}, f32[2,1,32,512]{3,2,1,0:T(8,128)S(1)}, u32[]{:S(2)}, u32[]{:S(2)}) %collective-permute-start.7) | collective-permute-done | bytes 131104 | tf_op jit(solution)/shard_map/ppermute | solution.py:15
  63.4 0.9 convolution_bitcast_fusion.20
  64.7 1.9 %collective-permute-start.9 = (f32[2,1,32,512]{3,2,1,0:T(8,128)S(1)}, f32[2,1,32,512]{3,2,1,0:T(8,128)S(1)}, u32[]{:S(2)}, u32[]{:S(2)}) collective-permute-start(f32[2,1,32,512]{3,2,1,0:T(8,128)S(1)} %constant_dynamic-update-slice_fusion.2), channel_id=1, source_target_pairs={{0,8},{8,16},{16,24},{1,9},{9,17},{17,25},{2,10},{10,18},{18,26},{... | collective-permute-start | bytes 393224 | tf_op jit(solution)/shard_map/ppermute | solution.py:26
  69.0 1.3 collective-permute-start.11
  70.3 5.2 %collective-permute-start.10 = (f32[2,1,32,512]{3,2,1,0:T(8,128)S(1)}, f32[2,1,32,512]{3,2,1,0:T(8,128)S(1)}, u32[]{:S(2)}, u32[]{:S(2)}) collective-permute-start(f32[2,1,32,512]{3,2,1,0:T(8,128)S(1)} %pad_maximum_fusion.16), channel_id=1, source_target_pairs={{0,1},{1,2},{2,3},{3,4},{4,5},{5,6},{6,7},{8,9},{9,10},{10,11},{11... | collective-permute-start | bytes 393224 | tf_op jit(solution)/shard_map/ppermute | solution.py:15
  75.5 1.7 collective-permute-done.11
  77.2 3.7 %collective-permute-done.10 = f32[2,1,32,512]{3,2,1,0:T(8,128)S(1)} collective-permute-done((f32[2,1,32,512]{3,2,1,0:T(8,128)S(1)}, f32[2,1,32,512]{3,2,1,0:T(8,128)S(1)}, u32[]{:S(2)}, u32[]{:S(2)}) %collective-permute-start.10) | collective-permute-done | bytes 131104 | tf_op jit(solution)/shard_map/ppermute | solution.py:15
  83.0 1.3 collective-permute-start.13
  84.3 5.0 %collective-permute-start.12 = (f32[2,1,32,512]{3,2,1,0:T(8,128)S(1)}, f32[2,1,32,512]{3,2,1,0:T(8,128)S(1)}, u32[]{:S(2)}, u32[]{:S(2)}) collective-permute-start(f32[2,1,32,512]{3,2,1,0:T(8,128)S(1)} %pad_maximum_fusion.17), channel_id=1, source_target_pairs={{0,1},{1,2},{2,3},{3,4},{4,5},{5,6},{6,7},{8,9},{9,10},{10,11},{11... | collective-permute-start | bytes 393224 | tf_op jit(solution)/shard_map/ppermute | solution.py:15
  89.3 1.8 collective-permute-done.13
  91.1 3.0 %collective-permute-done.12 = f32[2,1,32,512]{3,2,1,0:T(8,128)S(1)} collective-permute-done((f32[2,1,32,512]{3,2,1,0:T(8,128)S(1)}, f32[2,1,32,512]{3,2,1,0:T(8,128)S(1)}, u32[]{:S(2)}, u32[]{:S(2)}) %collective-permute-start.12) | collective-permute-done | bytes 131104 | tf_op jit(solution)/shard_map/ppermute | solution.py:15
  94.7 0.9 convolution_bitcast_fusion.18
  95.9 1.9 %collective-permute-start.14 = (f32[2,1,32,512]{3,2,1,0:T(8,128)S(1)}, f32[2,1,32,512]{3,2,1,0:T(8,128)S(1)}, u32[]{:S(2)}, u32[]{:S(2)}) collective-permute-start(f32[2,1,32,512]{3,2,1,0:T(8,128)S(1)} %constant_dynamic-update-slice_fusion.4), channel_id=1, source_target_pairs={{0,8},{8,16},{16,24},{1,9},{9,17},{17,25},{2,10},{10,18},{18,26},{... | collective-permute-start | bytes 393224 | tf_op jit(solution)/shard_map/ppermute | solution.py:26
  100.2 1.3 collective-permute-start.16
  101.5 5.0 %collective-permute-start.15 = (f32[2,1,32,512]{3,2,1,0:T(8,128)S(1)}, f32[2,1,32,512]{3,2,1,0:T(8,128)S(1)}, u32[]{:S(2)}, u32[]{:S(2)}) collective-permute-start(f32[2,1,32,512]{3,2,1,0:T(8,128)S(1)} %pad_maximum_fusion.18), channel_id=1, source_target_pairs={{0,1},{1,2},{2,3},{3,4},{4,5},{5,6},{6,7},{8,9},{9,10},{10,11},{11... | collective-permute-start | bytes 393224 | tf_op jit(solution)/shard_map/ppermute | solution.py:15
  106.5 1.7 collective-permute-done.16
  108.3 3.0 %collective-permute-done.15 = f32[2,1,32,512]{3,2,1,0:T(8,128)S(1)} collective-permute-done((f32[2,1,32,512]{3,2,1,0:T(8,128)S(1)}, f32[2,1,32,512]{3,2,1,0:T(8,128)S(1)}, u32[]{:S(2)}, u32[]{:S(2)}) %collective-permute-start.15) | collective-permute-done | bytes 131104 | tf_op jit(solution)/shard_map/ppermute | solution.py:15
  111.9 0.9 convolution_bitcast_fusion.17
  113.4 1.3 collective-permute-start.18
  114.7 5.0 %collective-permute-start.17 = (f32[2,1,32,512]{3,2,1,0:T(8,128)S(1)}, f32[2,1,32,512]{3,2,1,0:T(8,128)S(1)}, u32[]{:S(2)}, u32[]{:S(2)}) collective-permute-start(f32[2,1,32,512]{3,2,1,0:T(8,128)S(1)} %pad_maximum_fusion.19), channel_id=1, source_target_pairs={{0,1},{1,2},{2,3},{3,4},{4,5},{5,6},{6,7},{8,9},{9,10},{10,11},{11... | collective-permute-start | bytes 393224 | tf_op jit(solution)/shard_map/ppermute | solution.py:15
  119.7 1.7 collective-permute-done.18
  121.4 3.0 %collective-permute-done.17 = f32[2,1,32,512]{3,2,1,0:T(8,128)S(1)} collective-permute-done((f32[2,1,32,512]{3,2,1,0:T(8,128)S(1)}, f32[2,1,32,512]{3,2,1,0:T(8,128)S(1)}, u32[]{:S(2)}, u32[]{:S(2)}) %collective-permute-start.17) | collective-permute-done | bytes 131104 | tf_op jit(solution)/shard_map/ppermute | solution.py:15
  125.1 0.9 convolution_bitcast_fusion.16
  126.3 1.9 %collective-permute-start.19 = (f32[2,1,32,512]{3,2,1,0:T(8,128)S(1)}, f32[2,1,32,512]{3,2,1,0:T(8,128)S(1)}, u32[]{:S(2)}, u32[]{:S(2)}) collective-permute-start(f32[2,1,32,512]{3,2,1,0:T(8,128)S(1)} %constant_dynamic-update-slice_fusion.6), channel_id=1, source_target_pairs={{0,8},{8,16},{16,24},{1,9},{9,17},{17,25},{2,10},{10,18},{18,26},{... | collective-permute-start | bytes 393224 | tf_op jit(solution)/shard_map/ppermute | solution.py:26
  130.2 1.3 collective-permute-start.21
  131.5 5.0 %collective-permute-start.20 = (f32[2,1,32,512]{3,2,1,0:T(8,128)S(1)}, f32[2,1,32,512]{3,2,1,0:T(8,128)S(1)}, u32[]{:S(2)}, u32[]{:S(2)}) collective-permute-start(f32[2,1,32,512]{3,2,1,0:T(8,128)S(1)} %pad_maximum_fusion.20), channel_id=1, source_target_pairs={{0,1},{1,2},{2,3},{3,4},{4,5},{5,6},{6,7},{8,9},{9,10},{10,11},{11... | collective-permute-start | bytes 393224 | tf_op jit(solution)/shard_map/ppermute | solution.py:15
  136.5 2.0 %collective-permute-done.21 = f32[2,1,32,512]{3,2,1,0:T(8,128)S(1)} collective-permute-done((f32[2,1,32,512]{3,2,1,0:T(8,128)S(1)}, f32[2,1,32,512]{3,2,1,0:T(8,128)S(1)}, u32[]{:S(2)}, u32[]{:S(2)}) %collective-permute-start.21) | collective-permute-done | bytes 131104 | tf_op jit(solution)/shard_map/ppermute | solution.py:18
  138.5 3.0 %collective-permute-done.20 = f32[2,1,32,512]{3,2,1,0:T(8,128)S(1)} collective-permute-done((f32[2,1,32,512]{3,2,1,0:T(8,128)S(1)}, f32[2,1,32,512]{3,2,1,0:T(8,128)S(1)}, u32[]{:S(2)}, u32[]{:S(2)}) %collective-permute-start.20) | collective-permute-done | bytes 131104 | tf_op jit(solution)/shard_map/ppermute | solution.py:15
  143.6 1.3 collective-permute-start.23
  144.9 5.0 %collective-permute-start.22 = (f32[2,1,32,512]{3,2,1,0:T(8,128)S(1)}, f32[2,1,32,512]{3,2,1,0:T(8,128)S(1)}, u32[]{:S(2)}, u32[]{:S(2)}) collective-permute-start(f32[2,1,32,512]{3,2,1,0:T(8,128)S(1)} %pad_maximum_fusion.21), channel_id=1, source_target_pairs={{0,1},{1,2},{2,3},{3,4},{4,5},{5,6},{6,7},{8,9},{9,10},{10,11},{11... | collective-permute-start | bytes 393224 | tf_op jit(solution)/shard_map/ppermute | solution.py:15
  149.9 1.8 collective-permute-done.23
  151.7 3.0 %collective-permute-done.22 = f32[2,1,32,512]{3,2,1,0:T(8,128)S(1)} collective-permute-done((f32[2,1,32,512]{3,2,1,0:T(8,128)S(1)}, f32[2,1,32,512]{3,2,1,0:T(8,128)S(1)}, u32[]{:S(2)}, u32[]{:S(2)}) %collective-permute-start.22) | collective-permute-done | bytes 131104 | tf_op jit(solution)/shard_map/ppermute | solution.py:15
  155.3 0.9 convolution_bitcast_fusion.14
  156.5 1.9 %collective-permute-start.24 = (f32[2,1,32,512]{3,2,1,0:T(8,128)S(1)}, f32[2,1,32,512]{3,2,1,0:T(8,128)S(1)}, u32[]{:S(2)}, u32[]{:S(2)}) collective-permute-start(f32[2,1,32,512]{3,2,1,0:T(8,128)S(1)} %constant_dynamic-update-slice_fusion.8), channel_id=1, source_target_pairs={{0,8},{8,16},{16,24},{1,9},{9,17},{17,25},{2,10},{10,18},{18,26},{... | collective-permute-start | bytes 393224 | tf_op jit(solution)/shard_map/ppermute | solution.py:26
  160.7 1.3 collective-permute-start.26
  162.0 5.2 %collective-permute-start.25 = (f32[2,1,32,512]{3,2,1,0:T(8,128)S(1)}, f32[2,1,32,512]{3,2,1,0:T(8,128)S(1)}, u32[]{:S(2)}, u32[]{:S(2)}) collective-permute-start(f32[2,1,32,512]{3,2,1,0:T(8,128)S(1)} %pad_maximum_fusion.22), channel_id=1, source_target_pairs={{0,1},{1,2},{2,3},{3,4},{4,5},{5,6},{6,7},{8,9},{9,10},{10,11},{11... | collective-permute-start | bytes 393224 | tf_op jit(solution)/shard_map/ppermute | solution.py:15
  167.3 1.5 collective-permute-done.26
  168.8 3.0 %collective-permute-done.25 = f32[2,1,32,512]{3,2,1,0:T(8,128)S(1)} collective-permute-done((f32[2,1,32,512]{3,2,1,0:T(8,128)S(1)}, f32[2,1,32,512]{3,2,1,0:T(8,128)S(1)}, u32[]{:S(2)}, u32[]{:S(2)}) %collective-permute-start.25) | collective-permute-done | bytes 131104 | tf_op jit(solution)/shard_map/ppermute | solution.py:15
  172.4 0.9 convolution_bitcast_fusion.13
  173.9 1.3 collective-permute-start.28
  175.2 5.0 %collective-permute-start.27 = (f32[2,1,32,512]{3,2,1,0:T(8,128)S(1)}, f32[2,1,32,512]{3,2,1,0:T(8,128)S(1)}, u32[]{:S(2)}, u32[]{:S(2)}) collective-permute-start(f32[2,1,32,512]{3,2,1,0:T(8,128)S(1)} %pad_maximum_fusion.23), channel_id=1, source_target_pairs={{0,1},{1,2},{2,3},{3,4},{4,5},{5,6},{6,7},{8,9},{9,10},{10,11},{11... | collective-permute-start | bytes 393224 | tf_op jit(solution)/shard_map/ppermute | solution.py:15
  180.3 1.7 collective-permute-done.28
  182.0 3.0 %collective-permute-done.27 = f32[2,1,32,512]{3,2,1,0:T(8,128)S(1)} collective-permute-done((f32[2,1,32,512]{3,2,1,0:T(8,128)S(1)}, f32[2,1,32,512]{3,2,1,0:T(8,128)S(1)}, u32[]{:S(2)}, u32[]{:S(2)}) %collective-permute-start.27) | collective-permute-done | bytes 131104 | tf_op jit(solution)/shard_map/ppermute | solution.py:15
  185.6 0.9 convolution_bitcast_fusion.12
  186.8 0.9 select_select_fusion
  (219 shorter events, 18.4 us)
Async XLA Ops:
  4.6 13.5 %collective-permute-start.1 = (f32[2,1,32,512]{3,2,1,0:T(8,128)S(1)}, f32[2,1,32,512]{3,2,1,0:T(8,128)S(1)}, u32[]{:S(2)}, u32[]{:S(2)}) collective-permute-start(f32[2,1,32,512]{3,2,1,0:T(8,128)S(1)} %pad_maximum_fusion.12), channel_id=1, source_target_pairs={{1,0},{2,1},{3,2},{4,3},{5,4},{6,5},{7,6},{9,8},{10,9},{11,10},{12... | collective-permute-start | bytes 393224 | tf_op jit(solution)/shard_map/ppermute | solution.py:18
  5.9 12.2 %collective-permute-start = (f32[2,1,32,512]{3,2,1,0:T(8,128)S(1)}, f32[2,1,32,512]{3,2,1,0:T(8,128)S(1)}, u32[]{:S(2)}, u32[]{:S(2)}) collective-permute-start(f32[2,1,32,512]{3,2,1,0:T(8,128)S(1)} %pad_maximum_fusion.12), channel_id=1, source_target_pairs={{0,1},{1,2},{2,3},{3,4},{4,5},{5,6},{6,7},{8,9},{9,10},{10,11},{11... | collective-permute-start | bytes 393224 | tf_op jit(solution)/shard_map/ppermute | solution.py:15
  19.7 1.0 copy-start.1
  19.7 1.1 copy-start.2
  21.1 7.8 %collective-permute-start.3 = (f32[2,1,32,512]{3,2,1,0:T(8,128)S(1)}, f32[2,1,32,512]{3,2,1,0:T(8,128)S(1)}, u32[]{:S(2)}, u32[]{:S(2)}) collective-permute-start(f32[2,1,32,512]{3,2,1,0:T(8,128)S(1)} %pad_maximum_fusion.13), channel_id=1, source_target_pairs={{1,0},{2,1},{3,2},{4,3},{5,4},{6,5},{7,6},{9,8},{10,9},{11,10},{12... | collective-permute-start | bytes 393224 | tf_op jit(solution)/shard_map/ppermute | solution.py:18
  22.4 9.4 %collective-permute-start.2 = (f32[2,1,32,512]{3,2,1,0:T(8,128)S(1)}, f32[2,1,32,512]{3,2,1,0:T(8,128)S(1)}, u32[]{:S(2)}, u32[]{:S(2)}) collective-permute-start(f32[2,1,32,512]{3,2,1,0:T(8,128)S(1)} %pad_maximum_fusion.13), channel_id=1, source_target_pairs={{0,1},{1,2},{2,3},{3,4},{4,5},{5,6},{6,7},{8,9},{9,10},{10,11},{11... | collective-permute-start | bytes 393224 | tf_op jit(solution)/shard_map/ppermute | solution.py:15
  33.4 3.9 %copy-start = (f32[2,3,32,512]{3,2,1,0:T(8,128)S(1)}, f32[2,3,32,512]{3,2,1,0:T(8,128)}, u32[]{:S(2)}) copy-start(f32[2,3,32,512]{3,2,1,0:T(8,128)} %param.4) | copy-start | bytes 1179652
  33.7 3.6 %collective-permute-start.4 = (f32[2,1,32,512]{3,2,1,0:T(8,128)S(1)}, f32[2,1,32,512]{3,2,1,0:T(8,128)S(1)}, u32[]{:S(2)}, u32[]{:S(2)}) collective-permute-start(f32[2,1,32,512]{3,2,1,0:T(8,128)S(1)} %constant_dynamic-update-slice_fusion), channel_id=1, source_target_pairs={{0,8},{8,16},{16,24},{1,9},{9,17},{17,25},{2,10},{10,18},{18,26},{... | collective-permute-start | bytes 393224 | tf_op jit(solution)/shard_map/ppermute | solution.py:26
  37.6 7.6 %collective-permute-start.6 = (f32[2,1,32,512]{3,2,1,0:T(8,128)S(1)}, f32[2,1,32,512]{3,2,1,0:T(8,128)S(1)}, u32[]{:S(2)}, u32[]{:S(2)}) collective-permute-start(f32[2,1,32,512]{3,2,1,0:T(8,128)S(1)} %pad_maximum_fusion.14), channel_id=1, source_target_pairs={{1,0},{2,1},{3,2},{4,3},{5,4},{6,5},{7,6},{9,8},{10,9},{11,10},{12... | collective-permute-start | bytes 393224 | tf_op jit(solution)/shard_map/ppermute | solution.py:18
  38.9 10.6 %collective-permute-start.5 = (f32[2,1,32,512]{3,2,1,0:T(8,128)S(1)}, f32[2,1,32,512]{3,2,1,0:T(8,128)S(1)}, u32[]{:S(2)}, u32[]{:S(2)}) collective-permute-start(f32[2,1,32,512]{3,2,1,0:T(8,128)S(1)} %pad_maximum_fusion.14), channel_id=1, source_target_pairs={{0,1},{1,2},{2,3},{3,4},{4,5},{5,6},{6,7},{8,9},{9,10},{10,11},{11... | collective-permute-start | bytes 393224 | tf_op jit(solution)/shard_map/ppermute | solution.py:15
  51.7 8.2 %collective-permute-start.8 = (f32[2,1,32,512]{3,2,1,0:T(8,128)S(1)}, f32[2,1,32,512]{3,2,1,0:T(8,128)S(1)}, u32[]{:S(2)}, u32[]{:S(2)}) collective-permute-start(f32[2,1,32,512]{3,2,1,0:T(8,128)S(1)} %pad_maximum_fusion.15), channel_id=1, source_target_pairs={{1,0},{2,1},{3,2},{4,3},{5,4},{6,5},{7,6},{9,8},{10,9},{11,10},{12... | collective-permute-start | bytes 393224 | tf_op jit(solution)/shard_map/ppermute | solution.py:18
  53.0 9.8 %collective-permute-start.7 = (f32[2,1,32,512]{3,2,1,0:T(8,128)S(1)}, f32[2,1,32,512]{3,2,1,0:T(8,128)S(1)}, u32[]{:S(2)}, u32[]{:S(2)}) collective-permute-start(f32[2,1,32,512]{3,2,1,0:T(8,128)S(1)} %pad_maximum_fusion.15), channel_id=1, source_target_pairs={{0,1},{1,2},{2,3},{3,4},{4,5},{5,6},{6,7},{8,9},{9,10},{10,11},{11... | collective-permute-start | bytes 393224 | tf_op jit(solution)/shard_map/ppermute | solution.py:15
  64.7 4.0 %collective-permute-start.9 = (f32[2,1,32,512]{3,2,1,0:T(8,128)S(1)}, f32[2,1,32,512]{3,2,1,0:T(8,128)S(1)}, u32[]{:S(2)}, u32[]{:S(2)}) collective-permute-start(f32[2,1,32,512]{3,2,1,0:T(8,128)S(1)} %constant_dynamic-update-slice_fusion.2), channel_id=1, source_target_pairs={{0,8},{8,16},{16,24},{1,9},{9,17},{17,25},{2,10},{10,18},{18,26},{... | collective-permute-start | bytes 393224 | tf_op jit(solution)/shard_map/ppermute | solution.py:26
  69.0 8.2 %collective-permute-start.11 = (f32[2,1,32,512]{3,2,1,0:T(8,128)S(1)}, f32[2,1,32,512]{3,2,1,0:T(8,128)S(1)}, u32[]{:S(2)}, u32[]{:S(2)}) collective-permute-start(f32[2,1,32,512]{3,2,1,0:T(8,128)S(1)} %pad_maximum_fusion.16), channel_id=1, source_target_pairs={{1,0},{2,1},{3,2},{4,3},{5,4},{6,5},{7,6},{9,8},{10,9},{11,10},{12... | collective-permute-start | bytes 393224 | tf_op jit(solution)/shard_map/ppermute | solution.py:18
  70.3 10.6 %collective-permute-start.10 = (f32[2,1,32,512]{3,2,1,0:T(8,128)S(1)}, f32[2,1,32,512]{3,2,1,0:T(8,128)S(1)}, u32[]{:S(2)}, u32[]{:S(2)}) collective-permute-start(f32[2,1,32,512]{3,2,1,0:T(8,128)S(1)} %pad_maximum_fusion.16), channel_id=1, source_target_pairs={{0,1},{1,2},{2,3},{3,4},{4,5},{5,6},{6,7},{8,9},{9,10},{10,11},{11... | collective-permute-start | bytes 393224 | tf_op jit(solution)/shard_map/ppermute | solution.py:15
  83.0 8.1 %collective-permute-start.13 = (f32[2,1,32,512]{3,2,1,0:T(8,128)S(1)}, f32[2,1,32,512]{3,2,1,0:T(8,128)S(1)}, u32[]{:S(2)}, u32[]{:S(2)}) collective-permute-start(f32[2,1,32,512]{3,2,1,0:T(8,128)S(1)} %pad_maximum_fusion.17), channel_id=1, source_target_pairs={{1,0},{2,1},{3,2},{4,3},{5,4},{6,5},{7,6},{9,8},{10,9},{11,10},{12... | collective-permute-start | bytes 393224 | tf_op jit(solution)/shard_map/ppermute | solution.py:18
  84.3 9.7 %collective-permute-start.12 = (f32[2,1,32,512]{3,2,1,0:T(8,128)S(1)}, f32[2,1,32,512]{3,2,1,0:T(8,128)S(1)}, u32[]{:S(2)}, u32[]{:S(2)}) collective-permute-start(f32[2,1,32,512]{3,2,1,0:T(8,128)S(1)} %pad_maximum_fusion.17), channel_id=1, source_target_pairs={{0,1},{1,2},{2,3},{3,4},{4,5},{5,6},{6,7},{8,9},{9,10},{10,11},{11... | collective-permute-start | bytes 393224 | tf_op jit(solution)/shard_map/ppermute | solution.py:15
  95.9 4.0 %collective-permute-start.14 = (f32[2,1,32,512]{3,2,1,0:T(8,128)S(1)}, f32[2,1,32,512]{3,2,1,0:T(8,128)S(1)}, u32[]{:S(2)}, u32[]{:S(2)}) collective-permute-start(f32[2,1,32,512]{3,2,1,0:T(8,128)S(1)} %constant_dynamic-update-slice_fusion.4), channel_id=1, source_target_pairs={{0,8},{8,16},{16,24},{1,9},{9,17},{17,25},{2,10},{10,18},{18,26},{... | collective-permute-start | bytes 393224 | tf_op jit(solution)/shard_map/ppermute | solution.py:26
  100.2 8.1 %collective-permute-start.16 = (f32[2,1,32,512]{3,2,1,0:T(8,128)S(1)}, f32[2,1,32,512]{3,2,1,0:T(8,128)S(1)}, u32[]{:S(2)}, u32[]{:S(2)}) collective-permute-start(f32[2,1,32,512]{3,2,1,0:T(8,128)S(1)} %pad_maximum_fusion.18), channel_id=1, source_target_pairs={{1,0},{2,1},{3,2},{4,3},{5,4},{6,5},{7,6},{9,8},{10,9},{11,10},{12... | collective-permute-start | bytes 393224 | tf_op jit(solution)/shard_map/ppermute | solution.py:18
  101.5 9.7 %collective-permute-start.15 = (f32[2,1,32,512]{3,2,1,0:T(8,128)S(1)}, f32[2,1,32,512]{3,2,1,0:T(8,128)S(1)}, u32[]{:S(2)}, u32[]{:S(2)}) collective-permute-start(f32[2,1,32,512]{3,2,1,0:T(8,128)S(1)} %pad_maximum_fusion.18), channel_id=1, source_target_pairs={{0,1},{1,2},{2,3},{3,4},{4,5},{5,6},{6,7},{8,9},{9,10},{10,11},{11... | collective-permute-start | bytes 393224 | tf_op jit(solution)/shard_map/ppermute | solution.py:15
  113.4 8.1 %collective-permute-start.18 = (f32[2,1,32,512]{3,2,1,0:T(8,128)S(1)}, f32[2,1,32,512]{3,2,1,0:T(8,128)S(1)}, u32[]{:S(2)}, u32[]{:S(2)}) collective-permute-start(f32[2,1,32,512]{3,2,1,0:T(8,128)S(1)} %pad_maximum_fusion.19), channel_id=1, source_target_pairs={{1,0},{2,1},{3,2},{4,3},{5,4},{6,5},{7,6},{9,8},{10,9},{11,10},{12... | collective-permute-start | bytes 393224 | tf_op jit(solution)/shard_map/ppermute | solution.py:18
  114.7 9.7 %collective-permute-start.17 = (f32[2,1,32,512]{3,2,1,0:T(8,128)S(1)}, f32[2,1,32,512]{3,2,1,0:T(8,128)S(1)}, u32[]{:S(2)}, u32[]{:S(2)}) collective-permute-start(f32[2,1,32,512]{3,2,1,0:T(8,128)S(1)} %pad_maximum_fusion.19), channel_id=1, source_target_pairs={{0,1},{1,2},{2,3},{3,4},{4,5},{5,6},{6,7},{8,9},{9,10},{10,11},{11... | collective-permute-start | bytes 393224 | tf_op jit(solution)/shard_map/ppermute | solution.py:15
  126.3 3.6 %collective-permute-start.19 = (f32[2,1,32,512]{3,2,1,0:T(8,128)S(1)}, f32[2,1,32,512]{3,2,1,0:T(8,128)S(1)}, u32[]{:S(2)}, u32[]{:S(2)}) collective-permute-start(f32[2,1,32,512]{3,2,1,0:T(8,128)S(1)} %constant_dynamic-update-slice_fusion.6), channel_id=1, source_target_pairs={{0,8},{8,16},{16,24},{1,9},{9,17},{17,25},{2,10},{10,18},{18,26},{... | collective-permute-start | bytes 393224 | tf_op jit(solution)/shard_map/ppermute | solution.py:26
  130.2 8.3 %collective-permute-start.21 = (f32[2,1,32,512]{3,2,1,0:T(8,128)S(1)}, f32[2,1,32,512]{3,2,1,0:T(8,128)S(1)}, u32[]{:S(2)}, u32[]{:S(2)}) collective-permute-start(f32[2,1,32,512]{3,2,1,0:T(8,128)S(1)} %pad_maximum_fusion.20), channel_id=1, source_target_pairs={{1,0},{2,1},{3,2},{4,3},{5,4},{6,5},{7,6},{9,8},{10,9},{11,10},{12... | collective-permute-start | bytes 393224 | tf_op jit(solution)/shard_map/ppermute | solution.py:18
  131.5 10.0 %collective-permute-start.20 = (f32[2,1,32,512]{3,2,1,0:T(8,128)S(1)}, f32[2,1,32,512]{3,2,1,0:T(8,128)S(1)}, u32[]{:S(2)}, u32[]{:S(2)}) collective-permute-start(f32[2,1,32,512]{3,2,1,0:T(8,128)S(1)} %pad_maximum_fusion.20), channel_id=1, source_target_pairs={{0,1},{1,2},{2,3},{3,4},{4,5},{5,6},{6,7},{8,9},{9,10},{10,11},{11... | collective-permute-start | bytes 393224 | tf_op jit(solution)/shard_map/ppermute | solution.py:15
  143.6 8.1 %collective-permute-start.23 = (f32[2,1,32,512]{3,2,1,0:T(8,128)S(1)}, f32[2,1,32,512]{3,2,1,0:T(8,128)S(1)}, u32[]{:S(2)}, u32[]{:S(2)}) collective-permute-start(f32[2,1,32,512]{3,2,1,0:T(8,128)S(1)} %pad_maximum_fusion.21), channel_id=1, source_target_pairs={{1,0},{2,1},{3,2},{4,3},{5,4},{6,5},{7,6},{9,8},{10,9},{11,10},{12... | collective-permute-start | bytes 393224 | tf_op jit(solution)/shard_map/ppermute | solution.py:18
  144.9 9.7 %collective-permute-start.22 = (f32[2,1,32,512]{3,2,1,0:T(8,128)S(1)}, f32[2,1,32,512]{3,2,1,0:T(8,128)S(1)}, u32[]{:S(2)}, u32[]{:S(2)}) collective-permute-start(f32[2,1,32,512]{3,2,1,0:T(8,128)S(1)} %pad_maximum_fusion.21), channel_id=1, source_target_pairs={{0,1},{1,2},{2,3},{3,4},{4,5},{5,6},{6,7},{8,9},{9,10},{10,11},{11... | collective-permute-start | bytes 393224 | tf_op jit(solution)/shard_map/ppermute | solution.py:15
  156.5 3.9 %collective-permute-start.24 = (f32[2,1,32,512]{3,2,1,0:T(8,128)S(1)}, f32[2,1,32,512]{3,2,1,0:T(8,128)S(1)}, u32[]{:S(2)}, u32[]{:S(2)}) collective-permute-start(f32[2,1,32,512]{3,2,1,0:T(8,128)S(1)} %constant_dynamic-update-slice_fusion.8), channel_id=1, source_target_pairs={{0,8},{8,16},{16,24},{1,9},{9,17},{17,25},{2,10},{10,18},{18,26},{... | collective-permute-start | bytes 393224 | tf_op jit(solution)/shard_map/ppermute | solution.py:26
  160.7 8.1 %collective-permute-start.26 = (f32[2,1,32,512]{3,2,1,0:T(8,128)S(1)}, f32[2,1,32,512]{3,2,1,0:T(8,128)S(1)}, u32[]{:S(2)}, u32[]{:S(2)}) collective-permute-start(f32[2,1,32,512]{3,2,1,0:T(8,128)S(1)} %pad_maximum_fusion.22), channel_id=1, source_target_pairs={{1,0},{2,1},{3,2},{4,3},{5,4},{6,5},{7,6},{9,8},{10,9},{11,10},{12... | collective-permute-start | bytes 393224 | tf_op jit(solution)/shard_map/ppermute | solution.py:18
  162.0 9.7 %collective-permute-start.25 = (f32[2,1,32,512]{3,2,1,0:T(8,128)S(1)}, f32[2,1,32,512]{3,2,1,0:T(8,128)S(1)}, u32[]{:S(2)}, u32[]{:S(2)}) collective-permute-start(f32[2,1,32,512]{3,2,1,0:T(8,128)S(1)} %pad_maximum_fusion.22), channel_id=1, source_target_pairs={{0,1},{1,2},{2,3},{3,4},{4,5},{5,6},{6,7},{8,9},{9,10},{10,11},{11... | collective-permute-start | bytes 393224 | tf_op jit(solution)/shard_map/ppermute | solution.py:15
  173.9 8.1 %collective-permute-start.28 = (f32[2,1,32,512]{3,2,1,0:T(8,128)S(1)}, f32[2,1,32,512]{3,2,1,0:T(8,128)S(1)}, u32[]{:S(2)}, u32[]{:S(2)}) collective-permute-start(f32[2,1,32,512]{3,2,1,0:T(8,128)S(1)} %pad_maximum_fusion.23), channel_id=1, source_target_pairs={{1,0},{2,1},{3,2},{4,3},{5,4},{6,5},{7,6},{9,8},{10,9},{11,10},{12... | collective-permute-start | bytes 393224 | tf_op jit(solution)/shard_map/ppermute | solution.py:18
  175.2 9.7 %collective-permute-start.27 = (f32[2,1,32,512]{3,2,1,0:T(8,128)S(1)}, f32[2,1,32,512]{3,2,1,0:T(8,128)S(1)}, u32[]{:S(2)}, u32[]{:S(2)}) collective-permute-start(f32[2,1,32,512]{3,2,1,0:T(8,128)S(1)} %pad_maximum_fusion.23), channel_id=1, source_target_pairs={{0,1},{1,2},{2,3},{3,4},{4,5},{5,6},{6,7},{8,9},{9,10},{10,11},{11... | collective-permute-start | bytes 393224 | tf_op jit(solution)/shard_map/ppermute | solution.py:15
where the time goes:
time: 190 us; the launch traced here: 188 us
  starting transfers between devices  86.5 us (46%)
  waiting for transfers between devices  52.6 us (28%)
  between operations  15.9 us (8%)
  matrix products  15.7 us (8%)
  other arithmetic  11.3 us (6%)
  local copies, waits for them, and re-layouts  5.83 us (3%)
    ppermute x12, starting transfers between devices, padded_2(): lax.ppermute(lax.slice_in_dim(block, block.shape[dim] - width, None, axis...  61.5 us
    ppermute x12, waiting for transfers between devices, padded_2(): lax.ppermute(lax.slice_in_dim(block, block.shape[dim] - width, None, axis...  34.6 us
    ppermute x12, waiting for transfers between devices, padded_2(): lax.ppermute(lax.slice_in_dim(block, 0, width, axis=dim), axis, backward)  17.9 us
    ppermute x12, starting transfers between devices, padded_2(): lax.ppermute(lax.slice_in_dim(block, 0, width, axis=dim), axis, backward)  15.5 us
    dot_general x12, matrix products, blur_columns(): jnp.dot(joined, cmat, precision=lax.Precision.HIGHEST, preferred_element_...  10.9 us
    ppermute x5, starting transfers between devices, passed_along(): lax.ppermute(value, axis, [(source, source + steps) for source in range(f...  9.43 us
    dot_general x12, matrix products, blur_rows(): jnp.einsum('oi,vic->voc', rmat, stacked, precision=lax.Precision.HIGHEST,...  4.73 us
    sub x12, other arithmetic, propagate(): field[0] * trans_re - field[1] * trans_im  4.24 us
  transfers between devices with their start and end apart: 29, of which 22 were waited for; matrix products, arithmetic and copies ran while one was open for 2% of the time, Pallas kernels for 0%

commit v1 on v0

v1 whole, which is shorter than its diff:
```python
import functools

import jax
import jax.numpy as jnp
import ml_dtypes
import numpy as np
from jax import lax
from jax.experimental import pallas as pl
from jax.experimental.pallas import tpu as pltpu
from jax.sharding import PartitionSpec as P

HALF = 32
LANES = 128
PAIR = 2
MESH = pl.DeviceIdType.MESH

SIN_TERMS = (
    3.1415926535897931,
    -5.1677127800499694,
    2.5501640398773450,
    -0.59926452932079199,
    0.082145886611128236,
    -0.0073704309457143504,
    0.00046630280576761250,
)
COS_TERMS = (
    1.0,
    -4.9348022005446790,
    4.0587121264167676,
    -1.3352627688545893,
    0.23533063035889312,
    -0.025806891390014061,
    0.0019295743094039231,
    -0.00010463810492484570,
)


def series(square, terms):
    total = jnp.full_like(square, terms[-1])
    for term in terms[-2::-1]:
        total = total * square + term
    return total


def taps(offset, half):
    grid = np.arange(-half, half + 1, dtype=np.float64)
    norm = np.abs(
        np.sum((0.75 + 0.25 * np.cos(np.pi * grid / (half + 1))) * np.exp(1j * np.pi * grid**2 / (6.25 * half)))
    )
    place = offset.astype(np.float64)
    value = (0.75 + 0.25 * np.cos(np.pi * place / (half + 1))) * np.exp(1j * np.pi * place**2 / (6.25 * half))
    value = np.where(np.abs(offset) <= half, value / norm, 0.0)
    return value.real, value.imag


def in_two(matrix):
    matrix = matrix.astype(np.float32)
    high = matrix.astype(ml_dtypes.bfloat16)
    low = (matrix - high.astype(np.float32)).astype(ml_dtypes.bfloat16)
    return high, low


def row_matrix(rows, half):
    target, source = np.mgrid[0:rows, 0 : rows + 2 * half]
    real_part, imag_part = taps(source - half - target, half)
    return np.block([[real_part, -imag_part], [imag_part, real_part]])


def column_matrix(block, edge, half):
    source, target = np.mgrid[0 : block + 2 * edge, 0:block]
    real_part, imag_part = taps(source - edge - target, half)
    return np.block([[real_part, imag_part], [-imag_part, real_part]])


def split(value):
    high = value.astype(jnp.bfloat16)
    low = (value - high.astype(jnp.float32)).astype(jnp.bfloat16)
    return high, low


def dot(a, b):
    return jnp.dot(a, b, preferred_element_type=jnp.float32)


def body(
    depths, tiles, views, rows, cols, per_slab,
    incident_ref, delta_ref, beta_ref, rmat_ref, cmat_ref, out_ref,
    start_buf, volume, wave, field, trans, leaving,
    start_send, start_recv, vol_send, vol_recv, rim_send, rim_recv, out_send, out_recv,
):
    half = HALF
    span = PAIR * rows
    slices = depths * per_slab
    blocks = cols // LANES
    edge = LANES // 2
    d = lax.axis_index("depth")
    t = lax.axis_index("tile")
    pair = t // PAIR
    q = t % PAIR
    pairs = tiles // PAIR
    mine = (d // 2) * PAIR + q
    works = (d % 2 == 0) & (mine < views)
    places = [((v // PAIR) * 2, v % PAIR) for v in range(views)]

    barrier = pltpu.get_barrier_semaphore()
    for dd in range(depths):
        for qq in range(PAIR):
            here = (d == dd) & (q == qq)
            peer = (dd, pair * PAIR + qq)
            if (dd, qq) in places:

                @pl.when(jnp.logical_not(here))
                def _():
                    pl.semaphore_signal(barrier, inc=1, device_id=peer, device_id_type=MESH)
            else:

                @pl.when(works)
                def _():
                    pl.semaphore_signal(barrier, inc=1, device_id=peer, device_id_type=MESH)

    has_up = works & (pair > 0)
    has_down = works & (pair < pairs - 1)
    up = (d, jnp.maximum(t - PAIR, 0))
    down = (d, jnp.minimum(t + PAIR, tiles - 1))

    @pl.when(has_up)
    def _():
        pl.semaphore_signal(barrier, inc=1, device_id=up, device_id_type=MESH)

    @pl.when(has_down)
    def _():
        pl.semaphore_signal(barrier, inc=1, device_id=down, device_id_type=MESH)

    peers = jnp.where(works, depths * PAIR - 1, views)
    pl.semaphore_wait(barrier, peers + has_up.astype(jnp.int32) + has_down.astype(jnp.int32))

    def piece_copy(ref, c, i, v, target):
        return pltpu.make_async_remote_copy(
            src_ref=ref.at[v, i],
            dst_ref=volume.at[d * per_slab + i, c, q],
            send_sem=vol_send.at[i, c, v],
            recv_sem=vol_recv.at[d * per_slab + i, c, q],
            device_id=target,
            device_id_type=MESH,
        )

    def start_copy(v, target):
        return pltpu.make_async_remote_copy(
            src_ref=incident_ref.at[:, v],
            dst_ref=start_buf.at[q],
            send_sem=start_send,
            recv_sem=start_recv.at[q],
            device_id=target,
            device_id_type=MESH,
        )

    for v, (dd, qq) in enumerate(places):
        target = (dd, pair * PAIR + qq)

        @pl.when((d == dd) & (q != qq))
        def _():
            start_copy(v, target).start()

        @pl.when((d == dd) & (q == qq))
        def _():
            pltpu.make_async_copy(incident_ref.at[:, v], start_buf.at[q], start_recv.at[q]).start()

    for i in range(per_slab):
        for v, (dd, qq) in enumerate(places):
            target = (dd, pair * PAIR + qq)
            here = (d == dd) & (q == qq)
            for c, ref in enumerate((delta_ref, beta_ref)):

                @pl.when(here)
                def _():
                    pltpu.make_async_copy(
                        ref.at[v, i], volume.at[d * per_slab + i, c, q], vol_recv.at[d * per_slab + i, c, q]
                    ).start()

                @pl.when(jnp.logical_not(here))
                def _():
                    piece_copy(ref, c, i, v, target).start()

    def out_copy(slab, qq):
        return pltpu.make_async_remote_copy(
            src_ref=leaving.at[slab, :, pl.ds(qq * rows, rows)],
            dst_ref=out_ref.at[:, mine, 0],
            send_sem=out_send.at[slab, qq],
            recv_sem=out_recv.at[mine],
            device_id=(slab, pair * PAIR + qq),
            device_id_type=MESH,
        )

    def rim_copy(s, side):
        first = half if side == 0 else span
        land = span + half if side == 0 else 0
        return pltpu.make_async_remote_copy(
            src_ref=wave.at[s, :, pl.ds(first, half)],
            dst_ref=wave.at[s, :, pl.ds(land, half)],
            send_sem=rim_send.at[s, side],
            recv_sem=rim_recv.at[s, 1 - side],
            device_id=up if side == 0 else down,
            device_id_type=MESH,
        )

    def rim_arrival(s, side):
        land = 0 if side == 0 else span + half
        ref = wave.at[s, :, pl.ds(land, half)]
        return pltpu.make_async_copy(ref, ref, rim_recv.at[s, side])

    def transmission(s):
        for c in range(2):
            for qq in range(PAIR):
                ref = volume.at[s, c, qq]
                pltpu.make_async_copy(ref, ref, vol_recv.at[s, c, qq]).wait()
        u = volume[s, 0].reshape(span, cols) - 0.5
        amp = jnp.exp(-volume[s, 1].reshape(span, cols))
        square = u * u
        trans[0] = -amp * (u * series(square, SIN_TERMS))
        trans[1] = -amp * series(square, COS_TERMS)

    @pl.when(works)
    def _():
        @pl.when(pair == 0)
        def _():
            wave[:, :, 0:half] = jnp.zeros((slices, 2, half, cols), jnp.float32)

        @pl.when(pair == pairs - 1)
        def _():
            wave[:, :, span + half :] = jnp.zeros((slices, 2, half, cols), jnp.float32)

        for qq in range(PAIR):
            pltpu.make_async_copy(start_buf.at[qq], start_buf.at[qq], start_recv.at[qq]).wait()
        for qq in range(PAIR):
            field[:, qq * rows : (qq + 1) * rows] = start_buf[qq]
        transmission(0)

        @pl.loop(0, slices)
        def _(s):
            wave[s, 0, half : half + span] = field[0] * trans[0] - field[1] * trans[1]
            wave[s, 1, half : half + span] = field[0] * trans[1] + field[1] * trans[0]

            @pl.when(has_up)
            def _():
                rim_copy(s, 0).start()

            @pl.when(has_down)
            def _():
                rim_copy(s, 1).start()

            @pl.when(s < slices - 1)
            def _():
                transmission(s + 1)

            @pl.when(has_up)
            def _():
                rim_arrival(s, 0).wait()

            @pl.when(has_down)
            def _():
                rim_arrival(s, 1).wait()

            high, low = split(wave[s].reshape(2 * (span + 2 * half), cols))
            both = dot(rmat_ref[...], high)
            count = 2 * span
            wide = both[:count] + both[count:] + dot(rmat_ref[:count], low)
            windows = []
            for part in range(2):
                padded = jnp.concatenate(
                    [wide[part * span : (part + 1) * span], jnp.zeros((span, LANES), jnp.float32)], axis=1
                )
                padded = pltpu.roll(padded, edge, 1)
                windows.append(
                    jnp.concatenate([padded[:, b * LANES : (b + 2) * LANES] for b in range(blocks)], axis=0)
                )
            high, low = split(jnp.concatenate(windows, axis=1))
            result = dot(high, cmat_ref[0]) + dot(low, cmat_ref[0]) + dot(high, cmat_ref[1])
            for part in range(2):
                for b in range(blocks):
                    field[part, :, b * LANES : (b + 1) * LANES] = result[
                        b * span : (b + 1) * span, part * LANES : (part + 1) * LANES
                    ]

            @pl.when(s % per_slab == per_slab - 1)
            def _():
                slab = s // per_slab
                leaving[slab] = field[...]
                for qq in range(PAIR):
                    here = (d == slab) & (q == qq)

                    @pl.when(here)
                    def _():
                        pltpu.make_async_copy(
                            leaving.at[slab, :, pl.ds(qq * rows, rows)], out_ref.at[:, mine, 0], out_recv.at[mine]
                        ).start()

                    @pl.when(jnp.logical_not(here))
                    def _():
                        out_copy(slab, qq).start()

    for v, (dd, qq) in enumerate(places):
        target = (dd, pair * PAIR + qq)
        here = (d == dd) & (q == qq)

        @pl.when((d == dd) & (q != qq))
        def _():
            start_copy(v, target).wait_send()

        @pl.when(jnp.logical_not(here))
        def _():
            for i in range(per_slab):
                for c, ref in enumerate((delta_ref, beta_ref)):
                    piece_copy(ref, c, i, v, target).wait_send()

    for v in range(views):
        ref = out_ref.at[:, v, 0]
        pltpu.make_async_copy(ref, ref, out_recv.at[v]).wait()

    @pl.when(works)
    def _():
        @pl.loop(0, slices)
        def _(s):
            @pl.when(has_up)
            def _():
                rim_copy(s, 0).wait_send()

            @pl.when(has_down)
            def _():
                rim_copy(s, 1).wait_send()

        @pl.loop(0, depths)
        def _(slab):
            for qq in range(PAIR):

                @pl.when(jnp.logical_not((d == slab) & (q == qq)))
                def _():
                    out_copy(slab, qq).wait_send()


def in_order(views, order_ref, value_ref, out_ref):
    for k in range(views):
        out_ref[:, k] = value_ref[:, order_ref[k]]


def per_device(depths, tiles, incident, delta, beta, view_order):
    half = HALF
    _, views, rows, cols = incident.shape
    per_slab = delta.shape[1]
    slices = per_slab * depths
    span = PAIR * rows
    edge = LANES // 2
    rmat = jnp.asarray(np.concatenate(in_two(row_matrix(span, half)), axis=0))
    cmat = jnp.asarray(np.stack(in_two(column_matrix(LANES, edge, half))))
    anywhere = pl.BlockSpec(memory_space=pl.ANY)
    vmem = pl.BlockSpec(memory_space=pltpu.VMEM)
    shape = jax.ShapeDtypeStruct((2, views, 1, rows, cols), jnp.float32)
    f32 = jnp.float32
    dma = pltpu.SemaphoreType.DMA
    by_view = pl.pallas_call(
        functools.partial(body, depths, tiles, views, rows, cols, per_slab),
        out_shape=shape,
        in_specs=[anywhere, anywhere, anywhere, vmem, vmem],
        out_specs=anywhere,
        scratch_shapes=[
            pltpu.VMEM((PAIR, 2, rows, cols), f32),
            pltpu.VMEM((slices, 2, PAIR, rows, cols), f32),
            pltpu.VMEM((slices, 2, span + 2 * half, cols), f32),
            pltpu.VMEM((2, span, cols), f32),
            pltpu.VMEM((2, span, cols), f32),
            pltpu.VMEM((depths, 2, span, cols), f32),
            dma,
            dma((PAIR,)),
            dma((per_slab, 2, views)),
            dma((slices, 2, PAIR)),
            dma((slices, 2)),
            dma((slices, 2)),
            dma((depths, PAIR)),
            dma((views,)),
        ],
        compiler_params=pltpu.CompilerParams(
            collective_id=0, has_side_effects=True, vmem_limit_bytes=40 * 1024 * 1024
        ),
        name="views_by_worker",
    )(incident, delta, beta, rmat, cmat)
    return pl.pallas_call(
        functools.partial(in_order, views),
        out_shape=shape,
        in_specs=[pl.BlockSpec(memory_space=pltpu.SMEM), vmem],
        out_specs=vmem,
        name="stored_order",
    )(view_order, by_view)


def solution(mesh):
    return jax.shard_map(
        functools.partial(per_device, mesh.shape["depth"], mesh.shape["tile"]),
        mesh=mesh,
        in_specs=(
            P(None, None, "tile", None),
            P(None, "depth", "tile", None),
            P(None, "depth", "tile", None),
            P(),
        ),
        out_specs=P(None, None, "depth", "tile", None),
        check_vma=False,
    )
```

time: 190 us -> 68.8 us (0.36); the launches traced: 188 us -> 68.5 us
  starting transfers between devices: 86.5 us -> 0 us
  Pallas kernels: 0 us -> 62.8 us
  waiting for transfers between devices: 52.6 us -> 0 us
  between operations: 15.9 us -> 0.02 us
  matrix products: 15.7 us -> 0 us
  other arithmetic: 11.3 us -> 0 us
    ppermute x29 -> x0, starting transfers between devices: 86.5 us -> none  [the longest x12 61.5 us: padded_2(): lax.ppermute(lax.slice_in_dim(block, block.shape[dim] - width, None, axis...]
    pallas_call x0 -> x2, Pallas kernels: none -> 62.8 us  [the longest x1 61.1 us: per_device(): pl.pallas_call(functools.partial(body, depths, tiles, views, rows, cols,...]
    ppermute x29 -> x0, waiting for transfers between devices: 52.6 us -> none  [the longest x12 34.6 us: padded_2(): lax.ppermute(lax.slice_in_dim(block, block.shape[dim] - width, None, axis...]
    dot_general x24 -> x0, matrix products: 15.7 us -> none  [the longest x12 10.9 us: blur_columns(): jnp.dot(joined, cmat, precision=lax.Precision.HIGHEST, preferred_element_...]
    unnamed x11 -> x12, local copies, waits for them, and re-layouts: 0.88 us -> 5.66 us
    sub x14 -> x0, other arithmetic: 4.25 us -> none  [the longest x12 4.24 us: propagate(): field[0] * trans_re - field[1] * trans_im]
    div x1 -> x0, other arithmetic: 2.45 us -> none  [tap_values(): imag_part = jnp.where(inside, shape_win * jnp.sin(turn), 0.0) / norm]
  transfers between devices with their start and end apart: 29 -> 0, of which waited for: 22 -> 0; matrix products, arithmetic and copies ran while one was open for 2% -> 0% of each run, Pallas kernels for 0% -> 0%
where the time goes in v1:
time: 68.8 us; the launch traced here: 68.5 us
  Pallas kernels  62.8 us (91%)
  local copies, waits for them, and re-layouts  5.66 us (8%)
    pallas_call x1, Pallas kernels, per_device(): pl.pallas_call(functools.partial(body, depths, tiles, views, rows, cols,...  61.1 us
    unnamed x12, local copies, waits for them, and re-layouts  5.66 us
    pallas_call x1, Pallas kernels, per_device(): pl.pallas_call(functools.partial(in_order, views), out_shape=shape, in_sp...  1.78 us

profile of v1, /device:TPU:0, one launch (start us, length us, event | category | flops | bytes accessed | tf_op | source)
XLA Modules:
  0.0 68.5 jit_solution(17201331423049289947)
XLA Ops:
  0.0 0.0 copy-start.1
  0.0 1.0 %copy-done.1 = bf16[2,512,256]{2,1,0:T(8,128)(2,1)S(1)} copy-done((bf16[2,512,256]{2,1,0:T(8,128)(2,1)S(1)}, bf16[2,512,256]{2,1,0:T(8,128)(2,1)}, u32[]{:S(2)}) %copy-start.1) | copy-done | bytes 524312
  1.0 0.0 copy-start.2
  1.0 1.0 %copy-done.2 = f32[2,3,32,512]{3,2,1,0:T(8,128)S(1)} copy-done((f32[2,3,32,512]{3,2,1,0:T(8,128)S(1)}, f32[2,3,32,512]{3,2,1,0:T(8,128)}, u32[]{:S(2)}) %copy-start.2) | copy-done | bytes 393240
  2.0 0.0 copy-start.3
  2.0 1.0 %copy-done.3 = f32[3,2,32,512]{3,2,1,0:T(8,128)S(1)} copy-done((f32[3,2,32,512]{3,2,1,0:T(8,128)S(1)}, f32[3,2,32,512]{3,2,1,0:T(8,128)}, u32[]{:S(2)}) %copy-start.3) | copy-done | bytes 393240
  3.0 0.0 copy-start.4
  3.0 1.0 %copy-done.4 = f32[3,2,32,512]{3,2,1,0:T(8,128)S(1)} copy-done((f32[3,2,32,512]{3,2,1,0:T(8,128)S(1)}, f32[3,2,32,512]{3,2,1,0:T(8,128)}, u32[]{:S(2)}) %copy-start.4) | copy-done | bytes 393240
  4.0 0.0 copy-start.5
  4.0 0.9 %copy-done.5 = bf16[256,256]{1,0:T(8,128)(2,1)S(1)} copy-done((bf16[256,256]{1,0:T(8,128)(2,1)S(1)}, bf16[256,256]{1,0:T(8,128)(2,1)}, u32[]{:S(2)}) %copy-start.5) | copy-done | bytes 131096
  4.9 61.1 %views_by_worker.1.value_ref = f32[2,3,1,32,512]{4,3,2,1,0:T(8,128)S(1)} custom-call(f32[2,3,32,512]{3,2,1,0:T(8,128)S(1)} %copy-done.2, f32[3,2,32,512]{3,2,1,0:T(8,128)S(1)} %copy-done.3, f32[3,2,32,512]{3,2,1,0:T(8,128)S(1)} %copy-done.4, bf16[256,256]{1,0:T(8,128)(2,1)S(1)} %copy-done.5, bf16[2,512,256]{2,1,0:T(8,128)(2,1)S(1)} %copy-done.1), custom_call_target="tpu_custom_call" | custom-call | tf_op jit(solution)/shard_map/views_by_worker/pallas_call | solution.py:359
  66.0 0.0 copy-start
  66.0 0.7 %copy-done = f32[2,3,1,32,512]{4,3,2,1,0:T(8,128)} copy-done((f32[2,3,1,32,512]{4,3,2,1,0:T(8,128)}, f32[2,3,1,32,512]{4,3,2,1,0:T(8,128)S(1)}, u32[]{:S(2)}) %copy-start) | copy-done | bytes 393240
  66.7 1.8 %stored_order.1 = f32[2,3,1,32,512]{4,3,2,1,0:T(8,128)} custom-call(s32[3]{0:T(128)} %order_ref.1, f32[2,3,1,32,512]{4,3,2,1,0:T(8,128)} %copy-done), custom_call_target="tpu_custom_call" | custom-call | tf_op jit(solution)/shard_map/stored_order/pallas_call | solution.py:385
Async XLA Ops:
  0.0 1.0 %copy-start.1 = (bf16[2,512,256]{2,1,0:T(8,128)(2,1)S(1)}, bf16[2,512,256]{2,1,0:T(8,128)(2,1)}, u32[]{:S(2)}) copy-start(bf16[2,512,256]{2,1,0:T(8,128)(2,1)} %constant.5.clone.cmat_ref) | copy-start | bytes 1572868
  1.0 1.0 %copy-start.2 = (f32[2,3,32,512]{3,2,1,0:T(8,128)S(1)}, f32[2,3,32,512]{3,2,1,0:T(8,128)}, u32[]{:S(2)}) copy-start(f32[2,3,32,512]{3,2,1,0:T(8,128)} %incident_ref.1) | copy-start | bytes 1179652
  2.0 1.0 %copy-start.3 = (f32[3,2,32,512]{3,2,1,0:T(8,128)S(1)}, f32[3,2,32,512]{3,2,1,0:T(8,128)}, u32[]{:S(2)}) copy-start(f32[3,2,32,512]{3,2,1,0:T(8,128)} %delta_ref.1) | copy-start | bytes 1179652
  3.0 1.0 %copy-start.4 = (f32[3,2,32,512]{3,2,1,0:T(8,128)S(1)}, f32[3,2,32,512]{3,2,1,0:T(8,128)}, u32[]{:S(2)}) copy-start(f32[3,2,32,512]{3,2,1,0:T(8,128)} %beta_ref.1) | copy-start | bytes 1179652
  4.0 0.9 %copy-start.5 = (bf16[256,256]{1,0:T(8,128)(2,1)S(1)}, bf16[256,256]{1,0:T(8,128)(2,1)}, u32[]{:S(2)}) copy-start(bf16[256,256]{1,0:T(8,128)(2,1)} %constant.4.clone.rmat_ref) | copy-start | bytes 393220
  66.0 0.7 %copy-start = (f32[2,3,1,32,512]{4,3,2,1,0:T(8,128)}, f32[2,3,1,32,512]{4,3,2,1,0:T(8,128)S(1)}, u32[]{:S(2)}) copy-start(f32[2,3,1,32,512]{4,3,2,1,0:T(8,128)S(1)} %views_by_worker.1.value_ref) | copy-start | bytes 1179652

commit v2 on v1

v2 whole, which is shorter than its diff:
```python
import functools

import jax
import jax.numpy as jnp
import ml_dtypes
import numpy as np
from jax import lax
from jax.experimental import pallas as pl
from jax.experimental.pallas import tpu as pltpu
from jax.sharding import PartitionSpec as P

HALF = 32
LANES = 128
PAIR = 2
PARTS = 2
MESH = pl.DeviceIdType.MESH

SIN_TERMS = (
    3.1415926535897931,
    -5.1677127800499694,
    2.5501640398773450,
    -0.59926452932079199,
    0.082145886611128236,
    -0.0073704309457143504,
    0.00046630280576761250,
)
COS_TERMS = (
    1.0,
    -4.9348022005446790,
    4.0587121264167676,
    -1.3352627688545893,
    0.23533063035889312,
    -0.025806891390014061,
    0.0019295743094039231,
    -0.00010463810492484570,
)


def series(square, terms):
    total = jnp.full_like(square, terms[-1])
    for term in terms[-2::-1]:
        total = total * square + term
    return total


def taps(offset, half):
    grid = np.arange(-half, half + 1, dtype=np.float64)
    norm = np.abs(
        np.sum((0.75 + 0.25 * np.cos(np.pi * grid / (half + 1))) * np.exp(1j * np.pi * grid**2 / (6.25 * half)))
    )
    place = offset.astype(np.float64)
    value = (0.75 + 0.25 * np.cos(np.pi * place / (half + 1))) * np.exp(1j * np.pi * place**2 / (6.25 * half))
    value = np.where(np.abs(offset) <= half, value / norm, 0.0)
    return value.real, value.imag


def in_two(matrix):
    matrix = matrix.astype(np.float32)
    high = matrix.astype(ml_dtypes.bfloat16)
    low = (matrix - high.astype(np.float32)).astype(ml_dtypes.bfloat16)
    return high, low


def row_matrix(rows, half):
    target, source = np.mgrid[0:rows, 0 : rows + 2 * half]
    real_part, imag_part = taps(source - half - target, half)
    return np.block([[real_part, -imag_part], [imag_part, real_part]])


def column_matrix(block, edge, half):
    source, target = np.mgrid[0 : block + 2 * edge, 0:block]
    real_part, imag_part = taps(source - edge - target, half)
    return np.block([[real_part, imag_part], [-imag_part, real_part]])


def split(value):
    high = value.astype(jnp.bfloat16)
    low = (value - high.astype(jnp.float32)).astype(jnp.bfloat16)
    return high, low


def dot(a, b):
    return jnp.dot(a, b, preferred_element_type=jnp.float32)


def transmitted(delta, beta):
    u = delta - 0.5
    amp = jnp.exp(-beta)
    square = u * u
    return -amp * (u * series(square, SIN_TERMS)), -amp * series(square, COS_TERMS)


def body(
    depths, tiles, views, rows, cols, per_slab,
    incident_ref, delta_ref, beta_ref, rmat_ref, cmat_ref, out_ref,
    loads, first, volume, wave, trans, leaving, rmat_buf, cmat_buf,
    load_sem, first_send, first_recv, vol_send, vol_recv, rim_send, rim_recv, out_send, out_recv, go,
):
    half = HALF
    span = PAIR * rows
    slices = depths * per_slab
    blocks = cols // LANES
    edge = LANES // 2
    d = lax.axis_index("depth")
    t = lax.axis_index("tile")
    pair = t // PAIR
    q = t % PAIR
    pairs = tiles // PAIR
    mine = (d // 2) * PAIR + q
    works = (d % 2 == 0) & (mine < views)
    places = [((v // PAIR) * 2, v % PAIR) for v in range(views)]

    taps_in = [
        pltpu.make_async_copy(rmat_ref, rmat_buf, load_sem.at[0]),
        pltpu.make_async_copy(cmat_ref, cmat_buf, load_sem.at[1]),
    ]
    first_in = [
        pltpu.make_async_copy(incident_ref.at[0], loads.at[0], load_sem.at[2]),
        pltpu.make_async_copy(incident_ref.at[1], loads.at[1], load_sem.at[3]),
        pltpu.make_async_copy(delta_ref.at[:, 0], loads.at[2], load_sem.at[4]),
        pltpu.make_async_copy(beta_ref.at[:, 0], loads.at[3], load_sem.at[5]),
    ]

    @pl.when(d == 0)
    def _():
        for copy in first_in:
            copy.start()

    @pl.when(works)
    def _():
        for copy in taps_in:
            copy.start()

    barrier = pltpu.get_barrier_semaphore()
    for dd in range(depths):
        for qq in range(PAIR):
            here = (d == dd) & (q == qq)
            peer = (dd, pair * PAIR + qq)
            if (dd, qq) in places:

                @pl.when(jnp.logical_not(here))
                def _():
                    pl.semaphore_signal(barrier, inc=1, device_id=peer, device_id_type=MESH)
            else:

                @pl.when(works)
                def _():
                    pl.semaphore_signal(barrier, inc=1, device_id=peer, device_id_type=MESH)

    has_up = works & (pair > 0)
    has_down = works & (pair < pairs - 1)
    up = (d, jnp.maximum(t - PAIR, 0))
    down = (d, jnp.minimum(t + PAIR, tiles - 1))

    @pl.when(has_up)
    def _():
        pl.semaphore_signal(barrier, inc=1, device_id=up, device_id_type=MESH)

    @pl.when(has_down)
    def _():
        pl.semaphore_signal(barrier, inc=1, device_id=down, device_id_type=MESH)

    peers = jnp.where(works, depths * PAIR - 1, views)
    pl.semaphore_wait(barrier, peers + has_up.astype(jnp.int32) + has_down.astype(jnp.int32))

    def piece_copy(i, c, v, target):
        return pltpu.make_async_remote_copy(
            src_ref=(delta_ref, beta_ref)[c].at[v, i],
            dst_ref=volume.at[d * per_slab + i, c, q],
            send_sem=vol_send.at[i, c, v],
            recv_sem=vol_recv.at[d * per_slab + i, c, q],
            device_id=target,
            device_id_type=MESH,
        )

    def send_pieces(i, v):
        dd, qq = places[v]
        here = (d == dd) & (q == qq)
        for c, ref in enumerate((delta_ref, beta_ref)):

            @pl.when(here)
            def _():
                pltpu.make_async_copy(
                    ref.at[v, i], volume.at[d * per_slab + i, c, q], vol_recv.at[d * per_slab + i, c, q]
                ).start()

            @pl.when(jnp.logical_not(here))
            def _():
                piece_copy(i, c, v, (dd, pair * PAIR + qq)).start()

    def first_copy(v):
        dd, qq = places[v]
        return pltpu.make_async_remote_copy(
            src_ref=first.at[v],
            dst_ref=wave.at[0, :, pl.ds(half + q * rows, rows)],
            send_sem=first_send.at[v],
            recv_sem=first_recv.at[q],
            device_id=(dd, pair * PAIR + qq),
            device_id_type=MESH,
        )

    @pl.when(d == 0)
    def _():
        for copy in first_in:
            copy.wait()
        for v, (dd, qq) in enumerate(places):
            real_part, imag_part = transmitted(loads[2, v], loads[3, v])
            first[v, 0] = loads[0, v] * real_part - loads[1, v] * imag_part
            first[v, 1] = loads[0, v] * imag_part + loads[1, v] * real_part
            here = (d == dd) & (q == qq)

            @pl.when(here)
            def _():
                pltpu.make_async_copy(
                    first.at[v], wave.at[0, :, pl.ds(half + q * rows, rows)], first_recv.at[q]
                ).start()

            @pl.when(jnp.logical_not(here))
            def _():
                first_copy(v).start()

        for v, (dd, qq) in enumerate(places):

            @pl.when(jnp.logical_not((d == dd) & (q == qq)))
            def _():
                first_copy(v).wait_send()

        for i in range(1, per_slab):
            for v in range(views):
                send_pieces(i, v)

    @pl.when((d > 0) & jnp.logical_not(works))
    def _():
        for v in range(views):
            pl.semaphore_wait(go.at[v], 1)
            for i in range(per_slab):
                send_pieces(i, v)

    def out_copy(slab, qq):
        return pltpu.make_async_remote_copy(
            src_ref=leaving.at[slab, :, pl.ds(qq * rows, rows)],
            dst_ref=out_ref.at[:, mine, 0],
            send_sem=out_send.at[slab, qq],
            recv_sem=out_recv.at[mine],
            device_id=(slab, pair * PAIR + qq),
            device_id_type=MESH,
        )

    wide_cols = cols // PARTS

    def rim_copy(s, side, h):
        first_row = half if side == 0 else span
        land = span + half if side == 0 else 0
        columns = pl.ds(h * wide_cols, wide_cols)
        return pltpu.make_async_remote_copy(
            src_ref=wave.at[s, :, pl.ds(first_row, half), columns],
            dst_ref=wave.at[s, :, pl.ds(land, half), columns],
            send_sem=rim_send.at[s, side, h],
            recv_sem=rim_recv.at[s, 1 - side, h],
            device_id=up if side == 0 else down,
            device_id_type=MESH,
        )

    def send_rims(s, h):
        @pl.when(has_up)
        def _():
            rim_copy(s, 0, h).start()

        @pl.when(has_down)
        def _():
            rim_copy(s, 1, h).start()

    def rim_arrival(s, side, h):
        land = 0 if side == 0 else span + half
        ref = wave.at[s, :, pl.ds(land, half), pl.ds(h * wide_cols, wide_cols)]
        return pltpu.make_async_copy(ref, ref, rim_recv.at[s, side, h])

    def transmission(s):
        for c in range(2):
            for qq in range(PAIR):
                ref = volume.at[s, c, qq]
                pltpu.make_async_copy(ref, ref, vol_recv.at[s, c, qq]).wait()
        trans[0], trans[1] = transmitted(volume[s, 0].reshape(span, cols), volume[s, 1].reshape(span, cols))

    @pl.when(works)
    def _():
        @pl.when(pair == 0)
        def _():
            wave[:, :, 0:half] = jnp.zeros((slices, 2, half, cols), jnp.float32)

        @pl.when(pair == pairs - 1)
        def _():
            wave[:, :, span + half :] = jnp.zeros((slices, 2, half, cols), jnp.float32)

        for copy in taps_in:
            copy.wait()
        for qq in range(PAIR):
            ref = wave.at[0, :, pl.ds(half + qq * rows, rows)]
            pltpu.make_async_copy(ref, ref, first_recv.at[qq]).wait()
        for h in range(PARTS):
            send_rims(0, h)

        @pl.loop(0, slices)
        def _(s):
            for dd in range(1, depths):

                @pl.when(s == max(0, (dd - 1) * per_slab - 1))
                def _():
                    for qq in range(PAIR):
                        if (dd, qq) in places:

                            @pl.when((d == dd) & (q == qq))
                            def _():
                                for i in range(per_slab):
                                    for v in range(views):
                                        send_pieces(i, v)
                        else:
                            pl.semaphore_signal(
                                go.at[mine], inc=1, device_id=(dd, pair * PAIR + qq), device_id_type=MESH
                            )

            @pl.when(s < slices - 1)
            def _():
                transmission(s + 1)

            count = 2 * span
            parts = []
            for h in range(PARTS):

                @pl.when(has_up)
                def _():
                    rim_arrival(s, 0, h).wait()

                @pl.when(has_down)
                def _():
                    rim_arrival(s, 1, h).wait()

                columns = slice(h * wide_cols, (h + 1) * wide_cols)
                high, low = split(wave[s, :, :, columns].reshape(2 * (span + 2 * half), wide_cols))
                both = dot(rmat_buf[...], high)
                parts.append(both[:count] + both[count:] + dot(rmat_buf[:count], low))
            padded = jnp.concatenate(parts + [jnp.zeros((count, LANES), jnp.float32)], axis=1)
            high, low = split(pltpu.roll(padded, edge, 1))
            per_part = blocks // PARTS
            for h in range(PARTS):
                mine_blocks = range(h * per_part, (h + 1) * per_part)

                def windows(value):
                    return jnp.concatenate(
                        [
                            jnp.concatenate(
                                [
                                    value[:span, b * LANES : (b + 2) * LANES],
                                    value[span:, b * LANES : (b + 2) * LANES],
                                ],
                                axis=1,
                            )
                            for b in mine_blocks
                        ],
                        axis=0,
                    )

                high_h = windows(high)
                result = dot(high_h, cmat_buf[0]) + dot(windows(low), cmat_buf[0]) + dot(high_h, cmat_buf[1])
                real_part, imag_part = [
                    jnp.concatenate(
                        [
                            result[k * span : (k + 1) * span, part * LANES : (part + 1) * LANES]
                            for k in range(per_part)
                        ],
                        axis=1,
                    )
                    for part in range(2)
                ]
                columns = slice(h * wide_cols, (h + 1) * wide_cols)

                @pl.when(s < slices - 1)
                def _():
                    trans_re, trans_im = trans[0, :, columns], trans[1, :, columns]
                    wave[s + 1, 0, half : half + span, columns] = real_part * trans_re - imag_part * trans_im
                    wave[s + 1, 1, half : half + span, columns] = real_part * trans_im + imag_part * trans_re
                    send_rims(s + 1, h)

                @pl.when(s % per_slab == per_slab - 1)
                def _():
                    leaving[s // per_slab, 0, :, columns] = real_part
                    leaving[s // per_slab, 1, :, columns] = imag_part

            @pl.when(s % per_slab == per_slab - 1)
            def _():
                slab = s // per_slab
                for qq in range(PAIR):
                    here = (d == slab) & (q == qq)

                    @pl.when(here)
                    def _():
                        pltpu.make_async_copy(
                            leaving.at[slab, :, pl.ds(qq * rows, rows)], out_ref.at[:, mine, 0], out_recv.at[mine]
                        ).start()

                    @pl.when(jnp.logical_not(here))
                    def _():
                        out_copy(slab, qq).start()

    for v, (dd, qq) in enumerate(places):
        target = (dd, pair * PAIR + qq)

        @pl.when(jnp.logical_not((d == dd) & (q == qq)))
        def _():
            for i in range(per_slab):
                for c in range(2):
                    if i == 0:

                        @pl.when(d > 0)
                        def _():
                            piece_copy(i, c, v, target).wait_send()
                    else:
                        piece_copy(i, c, v, target).wait_send()

    for v in range(views):
        ref = out_ref.at[:, v, 0]
        pltpu.make_async_copy(ref, ref, out_recv.at[v]).wait()

    @pl.when(works)
    def _():
        @pl.loop(0, slices)
        def _(s):
            for h in range(PARTS):

                @pl.when(has_up)
                def _():
                    rim_copy(s, 0, h).wait_send()

                @pl.when(has_down)
                def _():
                    rim_copy(s, 1, h).wait_send()

        @pl.loop(0, depths)
        def _(slab):
            for qq in range(PAIR):

                @pl.when(jnp.logical_not((d == slab) & (q == qq)))
                def _():
                    out_copy(slab, qq).wait_send()


def in_order(views, order_ref, value_ref, out_ref, sems):
    copies = [
        pltpu.make_async_copy(value_ref.at[:, order_ref[k]], out_ref.at[:, k], sems.at[k]) for k in range(views)
    ]
    for copy in copies:
        copy.start()
    for copy in copies:
        copy.wait()


def per_device(depths, tiles, incident, delta, beta, view_order):
    half = HALF
    _, views, rows, cols = incident.shape
    per_slab = delta.shape[1]
    slices = per_slab * depths
    span = PAIR * rows
    edge = LANES // 2
    rmat = jnp.asarray(np.concatenate(in_two(row_matrix(span, half)), axis=0))
    cmat = jnp.asarray(np.stack(in_two(column_matrix(LANES, edge, half))))
    anywhere = pl.BlockSpec(memory_space=pl.ANY)
    hbm = pl.BlockSpec(memory_space=pltpu.HBM)
    shape = jax.ShapeDtypeStruct((2, views, 1, rows, cols), jnp.float32)
    f32 = jnp.float32
    dma = pltpu.SemaphoreType.DMA
    by_view = pl.pallas_call(
        functools.partial(body, depths, tiles, views, rows, cols, per_slab),
        out_shape=shape,
        in_specs=[hbm] * 5,
        out_specs=anywhere,
        scratch_shapes=[
            pltpu.VMEM((4, views, rows, cols), f32),
            pltpu.VMEM((views, 2, rows, cols), f32),
            pltpu.VMEM((slices, 2, PAIR, rows, cols), f32),
            pltpu.VMEM((slices, 2, span + 2 * half, cols), f32),
            pltpu.VMEM((2, span, cols), f32),
            pltpu.VMEM((depths, 2, span, cols), f32),
            pltpu.VMEM(rmat.shape, rmat.dtype),
            pltpu.VMEM(cmat.shape, cmat.dtype),
            dma((6,)),
            dma((views,)),
            dma((PAIR,)),
            dma((per_slab, 2, views)),
            dma((slices, 2, PAIR)),
            dma((slices, 2, PARTS)),
            dma((slices, 2, PARTS)),
            dma((depths, PAIR)),
            dma((views,)),
            pltpu.SemaphoreType.REGULAR((views,)),
        ],
        compiler_params=pltpu.CompilerParams(
            collective_id=0, has_side_effects=True, vmem_limit_bytes=63 * 1024 * 1024
        ),
        name="views_by_worker",
    )(incident, delta, beta, rmat, cmat)
    return pl.pallas_call(
        functools.partial(in_order, views),
        out_shape=shape,
        in_specs=[pl.BlockSpec(memory_space=pltpu.SMEM), anywhere],
        out_specs=hbm,
        scratch_shapes=[dma((views,))],
        name="stored_order",
    )(view_order, by_view)


def solution(mesh):
    return jax.shard_map(
        functools.partial(per_device, mesh.shape["depth"], mesh.shape["tile"]),
        mesh=mesh,
        in_specs=(
            P(None, None, "tile", None),
            P(None, "depth", "tile", None),
            P(None, "depth", "tile", None),
            P(),
        ),
        out_specs=P(None, None, "depth", "tile", None),
        check_vma=False,
    )
```

time: 68.8 us -> 64.6 us (0.939)
  local copies, waits for them, and re-layouts: 5.66 us -> 0 us
  Pallas kernels: 62.8 us -> 64.5 us
    pallas_call x1, Pallas kernels: 1.78 us -> 13.7 us  [per_device(): pl.pallas_call(functools.partial(in_order, views), out_shape=shape, in_sp...]
    pallas_call x1, Pallas kernels: 61.1 us -> 50.8 us  [per_device(): pl.pallas_call(functools.partial(body, depths, tiles, views, rows, cols,...]
    unnamed x12 -> x0, local copies, waits for them, and re-layouts: 5.66 us -> none
where the time goes in v2:
time: 64.6 us; the launch traced here: 64.5 us
  Pallas kernels  64.5 us (100%)
    pallas_call x1, Pallas kernels, per_device(): pl.pallas_call(functools.partial(body, depths, tiles, views, rows, cols,...  50.8 us
    pallas_call x1, Pallas kernels, per_device(): pl.pallas_call(functools.partial(in_order, views), out_shape=shape, in_sp...  13.7 us

profile of v2, /device:TPU:0, one launch (start us, length us, event | category | flops | bytes accessed | tf_op | source)
XLA Modules:
  0.0 64.5 jit_solution(5615906644056429480)
XLA Ops:
  0.0 50.8 %views_by_worker.1.value_ref = f32[2,3,1,32,512]{4,3,2,1,0:T(8,128)} custom-call(f32[2,3,32,512]{3,2,1,0:T(8,128)} %incident_ref.1, f32[3,2,32,512]{3,2,1,0:T(8,128)} %delta_ref.1, f32[3,2,32,512]{3,2,1,0:T(8,128)} %beta_ref.1, bf16[256,256]{1,0:T(8,128)(2,1)} %constant.4.clone.rmat_ref, bf16[2,512,256]{2,1,0:T(8,128)(2,1)} %constant.5.clone.cmat_ref), custom_call_target="tpu_custom_call" | custom-call | tf_op jit(solution)/shard_map/views_by_worker/pallas_call | solution.py:471
  50.8 13.7 %stored_order.1 = f32[2,3,1,32,512]{4,3,2,1,0:T(8,128)} custom-call(s32[3]{0:T(128)} %order_ref.1, f32[2,3,1,32,512]{4,3,2,1,0:T(8,128)} %views_by_worker.1.value_ref), custom_call_target="tpu_custom_call" | custom-call | tf_op jit(solution)/shard_map/stored_order/pallas_call | solution.py:501

commit v3 on v2

--- a/solution.py
+++ b/solution.py
@@ -12,7 +12,7 @@
 HALF = 32
 LANES = 128
 PAIR = 2
-PARTS = 2
+GROUP = 2
 MESH = pl.DeviceIdType.MESH
 
 SIN_TERMS = (
@@ -160,6 +160,15 @@
     def _():
         pl.semaphore_signal(barrier, inc=1, device_id=down, device_id_type=MESH)
 
+    @pl.when(d == 0)
+    def _():
+        for copy in first_in:
+            copy.wait()
+        for v in range(views):
+            real_part, imag_part = transmitted(loads[2, v], loads[3, v])
+            first[v, 0] = loads[0, v] * real_part - loads[1, v] * imag_part
+            first[v, 1] = loads[0, v] * imag_part + loads[1, v] * real_part
+
     peers = jnp.where(works, depths * PAIR - 1, views)
     pl.semaphore_wait(barrier, peers + has_up.astype(jnp.int32) + has_down.astype(jnp.int32))
 
@@ -201,12 +210,7 @@
 
     @pl.when(d == 0)
     def _():
-        for copy in first_in:
-            copy.wait()
         for v, (dd, qq) in enumerate(places):
-            real_part, imag_part = transmitted(loads[2, v], loads[3, v])
-            first[v, 0] = loads[0, v] * real_part - loads[1, v] * imag_part
-            first[v, 1] = loads[0, v] * imag_part + loads[1, v] * real_part
             here = (d == dd) & (q == qq)
 
             @pl.when(here)
@@ -246,12 +250,11 @@
             device_id_type=MESH,
         )
 
-    wide_cols = cols // PARTS
 
     def rim_copy(s, side, h):
         first_row = half if side == 0 else span
         land = span + half if side == 0 else 0
-        columns = pl.ds(h * wide_cols, wide_cols)
+        columns = pl.ds(h * LANES, LANES)
         return pltpu.make_async_remote_copy(
             src_ref=wave.at[s, :, pl.ds(first_row, half), columns],
             dst_ref=wave.at[s, :, pl.ds(land, half), columns],
@@ -272,7 +275,7 @@
 
     def rim_arrival(s, side, h):
         land = 0 if side == 0 else span + half
-        ref = wave.at[s, :, pl.ds(land, half), pl.ds(h * wide_cols, wide_cols)]
+        ref = wave.at[s, :, pl.ds(land, half), pl.ds(h * LANES, LANES)]
         return pltpu.make_async_copy(ref, ref, rim_recv.at[s, side, h])
 
     def transmission(s):
@@ -297,7 +300,7 @@
         for qq in range(PAIR):
             ref = wave.at[0, :, pl.ds(half + qq * rows, rows)]
             pltpu.make_async_copy(ref, ref, first_recv.at[qq]).wait()
-        for h in range(PARTS):
+        for h in range(blocks):
             send_rims(0, h)
 
         @pl.loop(0, slices)
@@ -324,67 +327,75 @@
                 transmission(s + 1)
 
             count = 2 * span
-            parts = []
-            for h in range(PARTS):
-
-                @pl.when(has_up)
-                def _():
-                    rim_arrival(s, 0, h).wait()
-
-                @pl.when(has_down)
-                def _():
-                    rim_arrival(s, 1, h).wait()
-
-                columns = slice(h * wide_cols, (h + 1) * wide_cols)
-                high, low = split(wave[s, :, :, columns].reshape(2 * (span + 2 * half), wide_cols))
+
+            def rows_done(first_block, last_block):
+                for h in range(first_block, last_block):
+
+                    @pl.when(has_up)
+                    def _():
+                        rim_arrival(s, 0, h).wait()
+
+                    @pl.when(has_down)
+                    def _():
+                        rim_arrival(s, 1, h).wait()
+
+                width = (last_block - first_block) * LANES
+                columns = slice(first_block * LANES, last_block * LANES)
+                high, low = split(wave[s, :, :, columns].reshape(2 * (span + 2 * half), width))
                 both = dot(rmat_buf[...], high)
-                parts.append(both[:count] + both[count:] + dot(rmat_buf[:count], low))
-            padded = jnp.concatenate(parts + [jnp.zeros((count, LANES), jnp.float32)], axis=1)
-            high, low = split(pltpu.roll(padded, edge, 1))
-            per_part = blocks // PARTS
-            for h in range(PARTS):
-                mine_blocks = range(h * per_part, (h + 1) * per_part)
+                return both[:count] + both[count:] + dot(rmat_buf[:count], low)
+
+            def columns_done(first_block, last_block, pieces):
+                high, low = split(pltpu.roll(pieces, pieces.shape[1] - edge, 1))
 
                 def windows(value):
-                    return jnp.concatenate(
-                        [
-                            jnp.concatenate(
-                                [
-                                    value[:span, b * LANES : (b + 2) * LANES],
-                                    value[span:, b * LANES : (b + 2) * LANES],
-                                ],
-                                axis=1,
-                            )
-                            for b in mine_blocks
-                        ],
-                        axis=0,
-                    )
-
-                high_h = windows(high)
-                result = dot(high_h, cmat_buf[0]) + dot(windows(low), cmat_buf[0]) + dot(high_h, cmat_buf[1])
-                real_part, imag_part = [
-                    jnp.concatenate(
-                        [
-                            result[k * span : (k + 1) * span, part * LANES : (part + 1) * LANES]
-                            for k in range(per_part)
-                        ],
-                        axis=1,
-                    )
-                    for part in range(2)
+                    return [
+                        jnp.concatenate(
+                            [
+                                value[:span, k * LANES : (k + 2) * LANES],
+                                value[span:, k * LANES : (k + 2) * LANES],
+                            ],
+                            axis=1,
+                        )
+                        for k in range(last_block - first_block)
+                    ]
+
+                high, low = windows(high), windows(low)
+                height = span * len(high)
+                both = dot(jnp.concatenate(high + low, axis=0), cmat_buf[0])
+                result = both[:height] + both[height:] + dot(jnp.concatenate(high, axis=0), cmat_buf[1])
+                for k, block in enumerate(range(first_block, last_block)):
+                    real_part, imag_part = [
+                        result[k * span : (k + 1) * span, part * LANES : (part + 1) * LANES] for part in range(2)
+                    ]
+                    columns = slice(block * LANES, (block + 1) * LANES)
+
+                    @pl.when(s < slices - 1)
+                    def _():
+                        trans_re, trans_im = trans[0, :, columns], trans[1, :, columns]
+                        wave[s + 1, 0, half : half + span, columns] = real_part * trans_re - imag_part * trans_im
+                        wave[s + 1, 1, half : half + span, columns] = real_part * trans_im + imag_part * trans_re
+                        send_rims(s + 1, block)
+
+                    @pl.when(s % per_slab == per_slab - 1)
+                    def _():
+                        leaving[s // per_slab, 0, :, columns] = real_part
+                        leaving[s // per_slab, 1, :, columns] = imag_part
+
+            outside = jnp.zeros((count, LANES), jnp.float32)
+            made = []
+            for first_block in range(0, blocks, GROUP):
+                last_block = min(first_block + GROUP, blocks)
+                if len(made) < last_block:
+                    width = last_block - len(made)
+                    joined = rows_done(len(made), last_block)
+                    made += [joined[:, k * LANES : (k + 1) * LANES] for k in range(width)]
+                if len(made) < min(last_block + 1, blocks):
+                    made.append(rows_done(last_block, last_block + 1))
+                pieces = [
+                    made[k] if 0 <= k < blocks else outside for k in range(first_block - 1, last_block + 1)
                 ]
-                columns = slice(h * wide_cols, (h + 1) * wide_cols)
-
-                @pl.when(s < slices - 1)
-                def _():
-                    trans_re, trans_im = trans[0, :, columns], trans[1, :, columns]
-                    wave[s + 1, 0, half : half + span, columns] = real_part * trans_re - imag_part * trans_im
-                    wave[s + 1, 1, half : half + span, columns] = real_part * trans_im + imag_part * trans_re
-                    send_rims(s + 1, h)
-
-                @pl.when(s % per_slab == per_slab - 1)
-                def _():
-                    leaving[s // per_slab, 0, :, columns] = real_part
-                    leaving[s // per_slab, 1, :, columns] = imag_part
+                columns_done(first_block, last_block, jnp.concatenate(pieces, axis=1))
 
             @pl.when(s % per_slab == per_slab - 1)
             def _():
@@ -425,7 +436,7 @@
     def _():
         @pl.loop(0, slices)
         def _(s):
-            for h in range(PARTS):
+            for h in range(blocks):
 
                 @pl.when(has_up)
                 def _():
@@ -444,14 +455,9 @@
                     out_copy(slab, qq).wait_send()
 
 
-def in_order(views, order_ref, value_ref, out_ref, sems):
-    copies = [
-        pltpu.make_async_copy(value_ref.at[:, order_ref[k]], out_ref.at[:, k], sems.at[k]) for k in range(views)
-    ]
-    for copy in copies:
-        copy.start()
-    for copy in copies:
-        copy.wait()
+def in_order(views, order_ref, value_ref, out_ref):
+    for k in range(views):
+        out_ref[:, k] = value_ref[:, order_ref[k]]
 
 
 def per_device(depths, tiles, incident, delta, beta, view_order):
@@ -465,6 +471,7 @@
     cmat = jnp.asarray(np.stack(in_two(column_matrix(LANES, edge, half))))
     anywhere = pl.BlockSpec(memory_space=pl.ANY)
     hbm = pl.BlockSpec(memory_space=pltpu.HBM)
+    vmem = pl.BlockSpec(memory_space=pltpu.VMEM)
     shape = jax.ShapeDtypeStruct((2, views, 1, rows, cols), jnp.float32)
     f32 = jnp.float32
     dma = pltpu.SemaphoreType.DMA
@@ -487,8 +494,8 @@
             dma((PAIR,)),
             dma((per_slab, 2, views)),
             dma((slices, 2, PAIR)),
-            dma((slices, 2, PARTS)),
-            dma((slices, 2, PARTS)),
+            dma((slices, 2, cols // LANES)),
+            dma((slices, 2, cols // LANES)),
             dma((depths, PAIR)),
             dma((views,)),
             pltpu.SemaphoreType.REGULAR((views,)),
@@ -501,9 +508,8 @@
     return pl.pallas_call(
         functools.partial(in_order, views),
         out_shape=shape,
-        in_specs=[pl.BlockSpec(memory_space=pltpu.SMEM), anywhere],
-        out_specs=hbm,
-        scratch_shapes=[dma((views,))],
+        in_specs=[pl.BlockSpec(memory_space=pltpu.SMEM), vmem],
+        out_specs=vmem,
         name="stored_order",
     )(view_order, by_view)
 

time: 64.6 us -> 50.5 us (0.78)
  Pallas kernels: 64.5 us -> 50.3 us
    pallas_call x1, Pallas kernels: 13.7 us -> 1.78 us  [per_device(): pl.pallas_call(functools.partial(in_order, views), out_shape=shape, in_sp...]
    pallas_call x1, Pallas kernels: 50.8 us -> 48.5 us  [per_device(): pl.pallas_call(functools.partial(body, depths, tiles, views, rows, cols,...]
where the time goes in v3:
time: 50.5 us; the launch traced here: 50.3 us
  Pallas kernels  50.3 us (100%)
    pallas_call x1, Pallas kernels, per_device(): pl.pallas_call(functools.partial(body, depths, tiles, views, rows, cols,...  48.5 us
    pallas_call x1, Pallas kernels, per_device(): pl.pallas_call(functools.partial(in_order, views), out_shape=shape, in_sp...  1.78 us

profile of v3, /device:TPU:0, one launch (start us, length us, event | category | flops | bytes accessed | tf_op | source)
XLA Modules:
  0.0 50.3 jit_solution(3503320343510356351)
XLA Ops:
  0.0 48.5 %views_by_worker.1.value_ref = f32[2,3,1,32,512]{4,3,2,1,0:T(8,128)} custom-call(f32[2,3,32,512]{3,2,1,0:T(8,128)} %incident_ref.1, f32[3,2,32,512]{3,2,1,0:T(8,128)} %delta_ref.1, f32[3,2,32,512]{3,2,1,0:T(8,128)} %beta_ref.1, bf16[256,256]{1,0:T(8,128)(2,1)} %constant.4.clone.rmat_ref, bf16[2,512,256]{2,1,0:T(8,128)(2,1)} %constant.5.clone.cmat_ref), custom_call_target="tpu_custom_call" | custom-call | tf_op jit(solution)/shard_map/views_by_worker/pallas_call | solution.py:478
  48.5 1.8 %stored_order.1 = f32[2,3,1,32,512]{4,3,2,1,0:T(8,128)} custom-call(s32[3]{0:T(128)} %order_ref.1, f32[2,3,1,32,512]{4,3,2,1,0:T(8,128)} %views_by_worker.1.value_ref), custom_call_target="tpu_custom_call" | custom-call | tf_op jit(solution)/shard_map/stored_order/pallas_call | solution.py:508

commit v4 on v3

--- a/solution.py
+++ b/solution.py
@@ -13,6 +13,7 @@
 LANES = 128
 PAIR = 2
 GROUP = 2
+STRIP = 8
 MESH = pl.DeviceIdType.MESH
 
 SIN_TERMS = (
@@ -110,6 +111,13 @@
     works = (d % 2 == 0) & (mine < views)
     places = [((v // PAIR) * 2, v % PAIR) for v in range(views)]
 
+    def at_worker(v):
+        return (d == (v // PAIR) * 2) & (q == v % PAIR)
+
+    def worker(v):
+        return ((v // PAIR) * 2, pair * PAIR + v % PAIR)
+
+
     taps_in = [
         pltpu.make_async_copy(rmat_ref, rmat_buf, load_sem.at[0]),
         pltpu.make_async_copy(cmat_ref, cmat_buf, load_sem.at[1]),
@@ -164,54 +172,60 @@
     def _():
         for copy in first_in:
             copy.wait()
-        for v in range(views):
-            real_part, imag_part = transmitted(loads[2, v], loads[3, v])
-            first[v, 0] = loads[0, v] * real_part - loads[1, v] * imag_part
-            first[v, 1] = loads[0, v] * imag_part + loads[1, v] * real_part
+
+        @pl.loop(0, views)
+        def _(v):
+            @pl.loop(0, rows // STRIP)
+            def _(r):
+                strip = pl.ds(pl.multiple_of(r * STRIP, STRIP), STRIP)
+                real_part, imag_part = transmitted(loads[2, v, strip], loads[3, v, strip])
+                wave_re, wave_im = loads[0, v, strip], loads[1, v, strip]
+                first[v, 0, strip] = wave_re * real_part - wave_im * imag_part
+                first[v, 1, strip] = wave_re * imag_part + wave_im * real_part
 
     peers = jnp.where(works, depths * PAIR - 1, views)
     pl.semaphore_wait(barrier, peers + has_up.astype(jnp.int32) + has_down.astype(jnp.int32))
 
-    def piece_copy(i, c, v, target):
+    def piece_copy(i, c, v):
         return pltpu.make_async_remote_copy(
             src_ref=(delta_ref, beta_ref)[c].at[v, i],
             dst_ref=volume.at[d * per_slab + i, c, q],
             send_sem=vol_send.at[i, c, v],
             recv_sem=vol_recv.at[d * per_slab + i, c, q],
-            device_id=target,
+            device_id=worker(v),
             device_id_type=MESH,
         )
 
     def send_pieces(i, v):
-        dd, qq = places[v]
-        here = (d == dd) & (q == qq)
-        for c, ref in enumerate((delta_ref, beta_ref)):
-
-            @pl.when(here)
-            def _():
+        here = at_worker(v)
+
+        @pl.when(here)
+        def _():
+            for c, ref in enumerate((delta_ref, beta_ref)):
                 pltpu.make_async_copy(
                     ref.at[v, i], volume.at[d * per_slab + i, c, q], vol_recv.at[d * per_slab + i, c, q]
                 ).start()
 
-            @pl.when(jnp.logical_not(here))
-            def _():
-                piece_copy(i, c, v, (dd, pair * PAIR + qq)).start()
+        @pl.when(jnp.logical_not(here))
+        def _():
+            for c in range(2):
+                piece_copy(i, c, v).start()
 
     def first_copy(v):
-        dd, qq = places[v]
         return pltpu.make_async_remote_copy(
             src_ref=first.at[v],
             dst_ref=wave.at[0, :, pl.ds(half + q * rows, rows)],
             send_sem=first_send.at[v],
             recv_sem=first_recv.at[q],
-            device_id=(dd, pair * PAIR + qq),
+            device_id=worker(v),
             device_id_type=MESH,
         )
 
     @pl.when(d == 0)
     def _():
-        for v, (dd, qq) in enumerate(places):
-            here = (d == dd) & (q == qq)
+        @pl.loop(0, views)
+        def _(v):
+            here = at_worker(v)
 
             @pl.when(here)
             def _():
@@ -223,21 +237,24 @@
             def _():
                 first_copy(v).start()
 
-        for v, (dd, qq) in enumerate(places):
-
-            @pl.when(jnp.logical_not((d == dd) & (q == qq)))
+        @pl.loop(0, views)
+        def _(v):
+            @pl.when(jnp.logical_not(at_worker(v)))
             def _():
                 first_copy(v).wait_send()
 
-        for i in range(1, per_slab):
-            for v in range(views):
-                send_pieces(i, v)
+        @pl.loop(0, (per_slab - 1) * views)
+        def _(k):
+            send_pieces(1 + k // views, k % views)
 
     @pl.when((d > 0) & jnp.logical_not(works))
     def _():
-        for v in range(views):
+        @pl.loop(0, views)
+        def _(v):
             pl.semaphore_wait(go.at[v], 1)
-            for i in range(per_slab):
+
+            @pl.loop(0, per_slab)
+            def _(i):
                 send_pieces(i, v)
 
     def out_copy(slab, qq):
@@ -283,17 +300,30 @@
             for qq in range(PAIR):
                 ref = volume.at[s, c, qq]
                 pltpu.make_async_copy(ref, ref, vol_recv.at[s, c, qq]).wait()
-        trans[0], trans[1] = transmitted(volume[s, 0].reshape(span, cols), volume[s, 1].reshape(span, cols))
+        for qq in range(PAIR):
+
+            @pl.loop(0, rows // STRIP)
+            def _(r):
+                strip = pl.ds(pl.multiple_of(r * STRIP, STRIP), STRIP)
+                land = pl.ds(pl.multiple_of(qq * rows + r * STRIP, STRIP), STRIP)
+                real_part, imag_part = transmitted(volume[s, 0, qq, strip], volume[s, 1, qq, strip])
+                trans[0, land] = real_part
+                trans[1, land] = imag_part
 
     @pl.when(works)
     def _():
+        def clear(first_row):
+            @pl.loop(0, slices)
+            def _(s):
+                wave[s, :, first_row : first_row + half] = jnp.zeros((2, half, cols), jnp.float32)
+
         @pl.when(pair == 0)
         def _():
-            wave[:, :, 0:half] = jnp.zeros((slices, 2, half, cols), jnp.float32)
+            clear(0)
 
         @pl.when(pair == pairs - 1)
         def _():
-            wave[:, :, span + half :] = jnp.zeros((slices, 2, half, cols), jnp.float32)
+            clear(span + half)
 
         for copy in taps_in:
             copy.wait()
@@ -314,9 +344,9 @@
 
                             @pl.when((d == dd) & (q == qq))
                             def _():
-                                for i in range(per_slab):
-                                    for v in range(views):
-                                        send_pieces(i, v)
+                                @pl.loop(0, per_slab * views)
+                                def _(k):
+                                    send_pieces(k // views, k % views)
                         else:
                             pl.semaphore_signal(
                                 go.at[mine], inc=1, device_id=(dd, pair * PAIR + qq), device_id_type=MESH
@@ -413,20 +443,14 @@
                     def _():
                         out_copy(slab, qq).start()
 
-    for v, (dd, qq) in enumerate(places):
-        target = (dd, pair * PAIR + qq)
-
-        @pl.when(jnp.logical_not((d == dd) & (q == qq)))
-        def _():
-            for i in range(per_slab):
-                for c in range(2):
-                    if i == 0:
-
-                        @pl.when(d > 0)
-                        def _():
-                            piece_copy(i, c, v, target).wait_send()
-                    else:
-                        piece_copy(i, c, v, target).wait_send()
+    @pl.loop(0, per_slab * views)
+    def _(k):
+        i, v = k // views, k % views
+
+        @pl.when(jnp.logical_not(at_worker(v)) & ((d > 0) | (i > 0)))
+        def _():
+            for c in range(2):
+                piece_copy(i, c, v).wait_send()
 
     for v in range(views):
         ref = out_ref.at[:, v, 0]
@@ -436,8 +460,8 @@
     def _():
         @pl.loop(0, slices)
         def _(s):
-            for h in range(blocks):
-
+            @pl.loop(0, blocks)
+            def _(h):
                 @pl.when(has_up)
                 def _():
                     rim_copy(s, 0, h).wait_send()

time: 50.5 us -> 50.6 us (level)
  no operation moved by 1% of the time
where the time goes in v4:
time: 50.6 us; the launch traced here: 50.5 us
  Pallas kernels  50.5 us (100%)
    pallas_call x1, Pallas kernels, per_device(): pl.pallas_call(functools.partial(body, depths, tiles, views, rows, cols,...  48.7 us
    pallas_call x1, Pallas kernels, per_device(): pl.pallas_call(functools.partial(in_order, views), out_shape=shape, in_sp...  1.78 us

profile of v4, /device:TPU:0, one launch (start us, length us, event | category | flops | bytes accessed | tf_op | source)
XLA Modules:
  0.0 50.5 jit_solution(11095896505224089636)
XLA Ops:
  0.0 48.7 %views_by_worker.1.value_ref = f32[2,3,1,32,512]{4,3,2,1,0:T(8,128)} custom-call(f32[2,3,32,512]{3,2,1,0:T(8,128)} %incident_ref.1, f32[3,2,32,512]{3,2,1,0:T(8,128)} %delta_ref.1, f32[3,2,32,512]{3,2,1,0:T(8,128)} %beta_ref.1, bf16[256,256]{1,0:T(8,128)(2,1)} %constant.4.clone.rmat_ref, bf16[2,512,256]{2,1,0:T(8,128)(2,1)} %constant.5.clone.cmat_ref), custom_call_target="tpu_custom_call" | custom-call | tf_op jit(solution)/shard_map/views_by_worker/pallas_call | solution.py:502
  48.7 1.8 %stored_order.1 = f32[2,3,1,32,512]{4,3,2,1,0:T(8,128)} custom-call(s32[3]{0:T(128)} %order_ref.1, f32[2,3,1,32,512]{4,3,2,1,0:T(8,128)} %views_by_worker.1.value_ref), custom_call_target="tpu_custom_call" | custom-call | tf_op jit(solution)/shard_map/stored_order/pallas_call | solution.py:532

commit v5 on v4

--- a/solution.py
+++ b/solution.py
@@ -243,11 +243,21 @@
             def _():
                 first_copy(v).wait_send()
 
+        pl.semaphore_signal(go.at[0], inc=1, device_id=(1, t), device_id_type=MESH)
+
         @pl.loop(0, (per_slab - 1) * views)
         def _(k):
             send_pieces(1 + k // views, k % views)
 
-    @pl.when((d > 0) & jnp.logical_not(works))
+    @pl.when(d == 1)
+    def _():
+        pl.semaphore_wait(go.at[0], 1)
+
+        @pl.loop(0, per_slab * views)
+        def _(k):
+            send_pieces(k // views, k % views)
+
+    @pl.when((d > 1) & jnp.logical_not(works))
     def _():
         @pl.loop(0, views)
         def _(v):
@@ -335,9 +345,9 @@
 
         @pl.loop(0, slices)
         def _(s):
-            for dd in range(1, depths):
-
-                @pl.when(s == max(0, (dd - 1) * per_slab - 1))
+            for dd in range(2, depths):
+
+                @pl.when(s == (dd - 2) * per_slab)
                 def _():
                     for qq in range(PAIR):
                         if (dd, qq) in places:

time: 50.6 us -> 52.1 us (1.030)
  Pallas kernels: 50.5 us -> 51.9 us
    pallas_call x1, Pallas kernels: 48.7 us -> 50.1 us  [per_device(): pl.pallas_call(functools.partial(body, depths, tiles, views, rows, cols,...]
where the time goes in v5:
time: 52.1 us; the launch traced here: 51.9 us
  Pallas kernels  51.9 us (100%)
    pallas_call x1, Pallas kernels, per_device(): pl.pallas_call(functools.partial(body, depths, tiles, views, rows, cols,...  50.1 us
    pallas_call x1, Pallas kernels, per_device(): pl.pallas_call(functools.partial(in_order, views), out_shape=shape, in_sp...  1.78 us

profile of v5, /device:TPU:0, one launch (start us, length us, event | category | flops | bytes accessed | tf_op | source)
XLA Modules:
  0.0 51.9 jit_solution(9284042286267726989)
XLA Ops:
  0.0 50.1 %views_by_worker.1.value_ref = f32[2,3,1,32,512]{4,3,2,1,0:T(8,128)} custom-call(f32[2,3,32,512]{3,2,1,0:T(8,128)} %incident_ref.1, f32[3,2,32,512]{3,2,1,0:T(8,128)} %delta_ref.1, f32[3,2,32,512]{3,2,1,0:T(8,128)} %beta_ref.1, bf16[256,256]{1,0:T(8,128)(2,1)} %constant.4.clone.rmat_ref, bf16[2,512,256]{2,1,0:T(8,128)(2,1)} %constant.5.clone.cmat_ref), custom_call_target="tpu_custom_call" | custom-call | tf_op jit(solution)/shard_map/views_by_worker/pallas_call | solution.py:512
  50.1 1.8 %stored_order.1 = f32[2,3,1,32,512]{4,3,2,1,0:T(8,128)} custom-call(s32[3]{0:T(128)} %order_ref.1, f32[2,3,1,32,512]{4,3,2,1,0:T(8,128)} %views_by_worker.1.value_ref), custom_call_target="tpu_custom_call" | custom-call | tf_op jit(solution)/shard_map/stored_order/pallas_call | solution.py:542

commit v6 on v4

--- a/solution.py
+++ b/solution.py
@@ -101,6 +101,8 @@
     span = PAIR * rows
     slices = depths * per_slab
     blocks = cols // LANES
+    groups = blocks // GROUP
+    wide_cols = GROUP * LANES
     edge = LANES // 2
     d = lax.axis_index("depth")
     t = lax.axis_index("tile")
@@ -271,7 +273,7 @@
     def rim_copy(s, side, h):
         first_row = half if side == 0 else span
         land = span + half if side == 0 else 0
-        columns = pl.ds(h * LANES, LANES)
+        columns = pl.ds(h * wide_cols, wide_cols)
         return pltpu.make_async_remote_copy(
             src_ref=wave.at[s, :, pl.ds(first_row, half), columns],
             dst_ref=wave.at[s, :, pl.ds(land, half), columns],
@@ -282,17 +284,17 @@
         )
 
     def send_rims(s, h):
-        @pl.when(has_up)
+        @pl.when(has_up & (s < slices))
         def _():
             rim_copy(s, 0, h).start()
 
-        @pl.when(has_down)
+        @pl.when(has_down & (s < slices))
         def _():
             rim_copy(s, 1, h).start()
 
     def rim_arrival(s, side, h):
         land = 0 if side == 0 else span + half
-        ref = wave.at[s, :, pl.ds(land, half), pl.ds(h * LANES, LANES)]
+        ref = wave.at[s, :, pl.ds(land, half), pl.ds(h * wide_cols, wide_cols)]
         return pltpu.make_async_copy(ref, ref, rim_recv.at[s, side, h])
 
     def transmission(s):
@@ -330,7 +332,7 @@
         for qq in range(PAIR):
             ref = wave.at[0, :, pl.ds(half + qq * rows, rows)]
             pltpu.make_async_copy(ref, ref, first_recv.at[qq]).wait()
-        for h in range(blocks):
+        for h in range(groups):
             send_rims(0, h)
 
         @pl.loop(0, slices)
@@ -358,20 +360,17 @@
 
             count = 2 * span
 
-            def rows_done(first_block, last_block):
-                for h in range(first_block, last_block):
-
-                    @pl.when(has_up)
-                    def _():
-                        rim_arrival(s, 0, h).wait()
-
-                    @pl.when(has_down)
-                    def _():
-                        rim_arrival(s, 1, h).wait()
-
-                width = (last_block - first_block) * LANES
-                columns = slice(first_block * LANES, last_block * LANES)
-                high, low = split(wave[s, :, :, columns].reshape(2 * (span + 2 * half), width))
+            def rows_done(h):
+                @pl.when(has_up)
+                def _():
+                    rim_arrival(s, 0, h).wait()
+
+                @pl.when(has_down)
+                def _():
+                    rim_arrival(s, 1, h).wait()
+
+                columns = slice(h * wide_cols, (h + 1) * wide_cols)
+                high, low = split(wave[s, :, :, columns].reshape(2 * (span + 2 * half), wide_cols))
                 both = dot(rmat_buf[...], high)
                 return both[:count] + both[count:] + dot(rmat_buf[:count], low)
 
@@ -399,33 +398,24 @@
                         result[k * span : (k + 1) * span, part * LANES : (part + 1) * LANES] for part in range(2)
                     ]
                     columns = slice(block * LANES, (block + 1) * LANES)
-
-                    @pl.when(s < slices - 1)
-                    def _():
-                        trans_re, trans_im = trans[0, :, columns], trans[1, :, columns]
-                        wave[s + 1, 0, half : half + span, columns] = real_part * trans_re - imag_part * trans_im
-                        wave[s + 1, 1, half : half + span, columns] = real_part * trans_im + imag_part * trans_re
-                        send_rims(s + 1, block)
-
-                    @pl.when(s % per_slab == per_slab - 1)
-                    def _():
-                        leaving[s // per_slab, 0, :, columns] = real_part
-                        leaving[s // per_slab, 1, :, columns] = imag_part
+                    trans_re, trans_im = trans[0, :, columns], trans[1, :, columns]
+                    wave[s + 1, 0, half : half + span, columns] = real_part * trans_re - imag_part * trans_im
+                    wave[s + 1, 1, half : half + span, columns] = real_part * trans_im + imag_part * trans_re
+                    leaving[s // per_slab, 0, :, columns] = real_part
+                    leaving[s // per_slab, 1, :, columns] = imag_part
 
             outside = jnp.zeros((count, LANES), jnp.float32)
             made = []
-            for first_block in range(0, blocks, GROUP):
-                last_block = min(first_block + GROUP, blocks)
-                if len(made) < last_block:
-                    width = last_block - len(made)
-                    joined = rows_done(len(made), last_block)
-                    made += [joined[:, k * LANES : (k + 1) * LANES] for k in range(width)]
-                if len(made) < min(last_block + 1, blocks):
-                    made.append(rows_done(last_block, last_block + 1))
+            for h in range(groups):
+                while len(made) < min((h + 1) * GROUP + 1, blocks):
+                    joined = rows_done(len(made) // GROUP)
+                    made += [joined[:, k * LANES : (k + 1) * LANES] for k in range(GROUP)]
+                first_block, last_block = h * GROUP, (h + 1) * GROUP
                 pieces = [
                     made[k] if 0 <= k < blocks else outside for k in range(first_block - 1, last_block + 1)
                 ]
                 columns_done(first_block, last_block, jnp.concatenate(pieces, axis=1))
+                send_rims(s + 1, h)
 
             @pl.when(s % per_slab == per_slab - 1)
             def _():
@@ -460,7 +450,7 @@
     def _():
         @pl.loop(0, slices)
         def _(s):
-            @pl.loop(0, blocks)
+            @pl.loop(0, groups)
             def _(h):
                 @pl.when(has_up)
                 def _():
@@ -508,7 +498,7 @@
             pltpu.VMEM((4, views, rows, cols), f32),
             pltpu.VMEM((views, 2, rows, cols), f32),
             pltpu.VMEM((slices, 2, PAIR, rows, cols), f32),
-            pltpu.VMEM((slices, 2, span + 2 * half, cols), f32),
+            pltpu.VMEM((slices + 1, 2, span + 2 * half, cols), f32),
             pltpu.VMEM((2, span, cols), f32),
             pltpu.VMEM((depths, 2, span, cols), f32),
             pltpu.VMEM(rmat.shape, rmat.dtype),
@@ -518,8 +508,8 @@
             dma((PAIR,)),
             dma((per_slab, 2, views)),
             dma((slices, 2, PAIR)),
-            dma((slices, 2, cols // LANES)),
-            dma((slices, 2, cols // LANES)),
+            dma((slices, 2, cols // (GROUP * LANES))),
+            dma((slices, 2, cols // (GROUP * LANES))),
             dma((depths, PAIR)),
             dma((views,)),
             pltpu.SemaphoreType.REGULAR((views,)),

time: 50.6 us -> 52.6 us (1.040)
  Pallas kernels: 50.5 us -> 52.4 us
    pallas_call x1, Pallas kernels: 48.7 us -> 50.6 us  [per_device(): pl.pallas_call(functools.partial(body, depths, tiles, views, rows, cols,...]
where the time goes in v6:
time: 52.6 us; the launch traced here: 52.4 us
  Pallas kernels  52.4 us (100%)
    pallas_call x1, Pallas kernels, per_device(): pl.pallas_call(functools.partial(body, depths, tiles, views, rows, cols,...  50.6 us
    pallas_call x1, Pallas kernels, per_device(): pl.pallas_call(functools.partial(in_order, views), out_shape=shape, in_sp...  1.78 us

profile of v6, /device:TPU:0, one launch (start us, length us, event | category | flops | bytes accessed | tf_op | source)
XLA Modules:
  0.0 52.4 jit_solution(16952375232283132805)
XLA Ops:
  0.0 50.6 %views_by_worker.1.value_ref = f32[2,3,1,32,512]{4,3,2,1,0:T(8,128)} custom-call(f32[2,3,32,512]{3,2,1,0:T(8,128)} %incident_ref.1, f32[3,2,32,512]{3,2,1,0:T(8,128)} %delta_ref.1, f32[3,2,32,512]{3,2,1,0:T(8,128)} %beta_ref.1, bf16[256,256]{1,0:T(8,128)(2,1)} %constant.4.clone.rmat_ref, bf16[2,512,256]{2,1,0:T(8,128)(2,1)} %constant.5.clone.cmat_ref), custom_call_target="tpu_custom_call" | custom-call | tf_op jit(solution)/shard_map/views_by_worker/pallas_call | solution.py:492
  50.6 1.8 %stored_order.1 = f32[2,3,1,32,512]{4,3,2,1,0:T(8,128)} custom-call(s32[3]{0:T(128)} %order_ref.1, f32[2,3,1,32,512]{4,3,2,1,0:T(8,128)} %views_by_worker.1.value_ref), custom_call_target="tpu_custom_call" | custom-call | tf_op jit(solution)/shard_map/stored_order/pallas_call | solution.py:522

commit v7 on v6

--- a/solution.py
+++ b/solution.py
@@ -12,7 +12,7 @@
 HALF = 32
 LANES = 128
 PAIR = 2
-GROUP = 2
+GROUP = 1
 STRIP = 8
 MESH = pl.DeviceIdType.MESH
 
@@ -101,8 +101,6 @@
     span = PAIR * rows
     slices = depths * per_slab
     blocks = cols // LANES
-    groups = blocks // GROUP
-    wide_cols = GROUP * LANES
     edge = LANES // 2
     d = lax.axis_index("depth")
     t = lax.axis_index("tile")
@@ -273,7 +271,7 @@
     def rim_copy(s, side, h):
         first_row = half if side == 0 else span
         land = span + half if side == 0 else 0
-        columns = pl.ds(h * wide_cols, wide_cols)
+        columns = pl.ds(h * LANES, LANES)
         return pltpu.make_async_remote_copy(
             src_ref=wave.at[s, :, pl.ds(first_row, half), columns],
             dst_ref=wave.at[s, :, pl.ds(land, half), columns],
@@ -283,18 +281,20 @@
             device_id_type=MESH,
         )
 
-    def send_rims(s, h):
+    def send_rims(s, first_block, last_block):
         @pl.when(has_up & (s < slices))
         def _():
-            rim_copy(s, 0, h).start()
+            for h in range(first_block, last_block):
+                rim_copy(s, 0, h).start()
 
         @pl.when(has_down & (s < slices))
         def _():
-            rim_copy(s, 1, h).start()
+            for h in range(first_block, last_block):
+                rim_copy(s, 1, h).start()
 
     def rim_arrival(s, side, h):
         land = 0 if side == 0 else span + half
-        ref = wave.at[s, :, pl.ds(land, half), pl.ds(h * wide_cols, wide_cols)]
+        ref = wave.at[s, :, pl.ds(land, half), pl.ds(h * LANES, LANES)]
         return pltpu.make_async_copy(ref, ref, rim_recv.at[s, side, h])
 
     def transmission(s):
@@ -332,8 +332,7 @@
         for qq in range(PAIR):
             ref = wave.at[0, :, pl.ds(half + qq * rows, rows)]
             pltpu.make_async_copy(ref, ref, first_recv.at[qq]).wait()
-        for h in range(groups):
-            send_rims(0, h)
+        send_rims(0, 0, blocks)
 
         @pl.loop(0, slices)
         def _(s):
@@ -360,17 +359,20 @@
 
             count = 2 * span
 
-            def rows_done(h):
+            def rows_done(first_block, last_block):
                 @pl.when(has_up)
                 def _():
-                    rim_arrival(s, 0, h).wait()
+                    for h in range(first_block, last_block):
+                        rim_arrival(s, 0, h).wait()
 
                 @pl.when(has_down)
                 def _():
-                    rim_arrival(s, 1, h).wait()
-
-                columns = slice(h * wide_cols, (h + 1) * wide_cols)
-                high, low = split(wave[s, :, :, columns].reshape(2 * (span + 2 * half), wide_cols))
+                    for h in range(first_block, last_block):
+                        rim_arrival(s, 1, h).wait()
+
+                columns = slice(first_block * LANES, last_block * LANES)
+                width = (last_block - first_block) * LANES
+                high, low = split(wave[s, :, :, columns].reshape(2 * (span + 2 * half), width))
                 both = dot(rmat_buf[...], high)
                 return both[:count] + both[count:] + dot(rmat_buf[:count], low)
 
@@ -406,16 +408,17 @@
 
             outside = jnp.zeros((count, LANES), jnp.float32)
             made = []
-            for h in range(groups):
-                while len(made) < min((h + 1) * GROUP + 1, blocks):
-                    joined = rows_done(len(made) // GROUP)
-                    made += [joined[:, k * LANES : (k + 1) * LANES] for k in range(GROUP)]
-                first_block, last_block = h * GROUP, (h + 1) * GROUP
+            for first_block in range(0, blocks, GROUP):
+                last_block = min(first_block + GROUP, blocks)
+                for wanted in (last_block, min(last_block + 1, blocks)):
+                    if len(made) < wanted:
+                        joined = rows_done(len(made), wanted)
+                        made += [joined[:, k : k + LANES] for k in range(0, joined.shape[1], LANES)]
                 pieces = [
                     made[k] if 0 <= k < blocks else outside for k in range(first_block - 1, last_block + 1)
                 ]
                 columns_done(first_block, last_block, jnp.concatenate(pieces, axis=1))
-                send_rims(s + 1, h)
+                send_rims(s + 1, first_block, last_block)
 
             @pl.when(s % per_slab == per_slab - 1)
             def _():
@@ -450,7 +453,7 @@
     def _():
         @pl.loop(0, slices)
         def _(s):
-            @pl.loop(0, groups)
+            @pl.loop(0, blocks)
             def _(h):
                 @pl.when(has_up)
                 def _():
@@ -508,8 +511,8 @@
             dma((PAIR,)),
             dma((per_slab, 2, views)),
             dma((slices, 2, PAIR)),
-            dma((slices, 2, cols // (GROUP * LANES))),
-            dma((slices, 2, cols // (GROUP * LANES))),
+            dma((slices, 2, cols // LANES)),
+            dma((slices, 2, cols // LANES)),
             dma((depths, PAIR)),
             dma((views,)),
             pltpu.SemaphoreType.REGULAR((views,)),

time: 52.6 us -> 49.6 us (0.943)
  Pallas kernels: 52.4 us -> 49.4 us
    pallas_call x1, Pallas kernels: 50.6 us -> 47.6 us  [per_device(): pl.pallas_call(functools.partial(body, depths, tiles, views, rows, cols,...]
where the time goes in v7:
time: 49.6 us; the launch traced here: 49.4 us
  Pallas kernels  49.4 us (100%)
    pallas_call x1, Pallas kernels, per_device(): pl.pallas_call(functools.partial(body, depths, tiles, views, rows, cols,...  47.6 us
    pallas_call x1, Pallas kernels, per_device(): pl.pallas_call(functools.partial(in_order, views), out_shape=shape, in_sp...  1.78 us

profile of v7, /device:TPU:0, one launch (start us, length us, event | category | flops | bytes accessed | tf_op | source)
XLA Modules:
  0.0 49.4 jit_solution(3098237423779001245)
XLA Ops:
  0.0 47.6 %views_by_worker.1.value_ref = f32[2,3,1,32,512]{4,3,2,1,0:T(8,128)} custom-call(f32[2,3,32,512]{3,2,1,0:T(8,128)} %incident_ref.1, f32[3,2,32,512]{3,2,1,0:T(8,128)} %delta_ref.1, f32[3,2,32,512]{3,2,1,0:T(8,128)} %beta_ref.1, bf16[256,256]{1,0:T(8,128)(2,1)} %constant.4.clone.rmat_ref, bf16[2,512,256]{2,1,0:T(8,128)(2,1)} %constant.5.clone.cmat_ref), custom_call_target="tpu_custom_call" | custom-call | tf_op jit(solution)/shard_map/views_by_worker/pallas_call | solution.py:495
  47.6 1.8 %stored_order.1 = f32[2,3,1,32,512]{4,3,2,1,0:T(8,128)} custom-call(s32[3]{0:T(128)} %order_ref.1, f32[2,3,1,32,512]{4,3,2,1,0:T(8,128)} %views_by_worker.1.value_ref), custom_call_target="tpu_custom_call" | custom-call | tf_op jit(solution)/shard_map/stored_order/pallas_call | solution.py:525

commit v8 on v7

--- a/solution.py
+++ b/solution.py
@@ -96,6 +96,7 @@
     incident_ref, delta_ref, beta_ref, rmat_ref, cmat_ref, out_ref,
     loads, first, volume, wave, trans, leaving, rmat_buf, cmat_buf,
     load_sem, first_send, first_recv, vol_send, vol_recv, rim_send, rim_recv, out_send, out_recv, go,
+    passing, passing_first, pass_send, pass_recv, pass_first_send, pass_first_recv,
 ):
     half = HALF
     span = PAIR * rows
@@ -139,7 +140,27 @@
         for copy in taps_in:
             copy.start()
 
+    relayed = None
+    for v, (dd, qq) in enumerate(places):
+        if dd >= 2 and PAIR == 2 and not any((dd + core, 1 - qq) in places for core in range(2)):
+            relayed = v
+            break
+    if relayed is None:
+        gives = passes = partners = jnp.bool_(False)
+        there = 0
+    else:
+        there, side = places[relayed]
+        gives = (d < 2) & (q != side)
+        passes = (d >= there) & (d < there + 2) & (q != side)
+        partners = (gives | passes) & (d % 2 == 1)
+
     barrier = pltpu.get_barrier_semaphore()
+
+    @pl.when(partners)
+    def _():
+        other = jnp.where(gives, d + there, d - there)
+        pl.semaphore_signal(barrier, inc=1, device_id=(other, t), device_id_type=MESH)
+
     for dd in range(depths):
         for qq in range(PAIR):
             here = (d == dd) & (q == qq)
@@ -183,7 +204,7 @@
                 first[v, 0, strip] = wave_re * real_part - wave_im * imag_part
                 first[v, 1, strip] = wave_re * imag_part + wave_im * real_part
 
-    peers = jnp.where(works, depths * PAIR - 1, views)
+    peers = jnp.where(works, depths * PAIR - 1, views) + partners.astype(jnp.int32)
     pl.semaphore_wait(barrier, peers + has_up.astype(jnp.int32) + has_down.astype(jnp.int32))
 
     def piece_copy(i, c, v):
@@ -196,8 +217,56 @@
             device_id_type=MESH,
         )
 
+    def by_relay(v):
+        return gives & (v == (-1 if relayed is None else relayed))
+
+    def piece_to_relay(i, c):
+        return pltpu.make_async_remote_copy(
+            src_ref=(delta_ref, beta_ref)[c].at[relayed or 0, i],
+            dst_ref=passing.at[i, c],
+            send_sem=vol_send.at[i, c, relayed or 0],
+            recv_sem=pass_recv.at[i, c],
+            device_id=(d + there, t),
+            device_id_type=MESH,
+        )
+
+    def piece_from_relay(i, c):
+        return pltpu.make_async_remote_copy(
+            src_ref=passing.at[i, c],
+            dst_ref=volume.at[(d - there) * per_slab + i, c, q],
+            send_sem=pass_send.at[i, c],
+            recv_sem=vol_recv.at[(d - there) * per_slab + i, c, q],
+            device_id=worker(relayed or 0),
+            device_id_type=MESH,
+        )
+
+    def first_to_relay():
+        return pltpu.make_async_remote_copy(
+            src_ref=first.at[relayed or 0],
+            dst_ref=passing_first,
+            send_sem=first_send.at[relayed or 0],
+            recv_sem=pass_first_recv,
+            device_id=(d + there, t),
+            device_id_type=MESH,
+        )
+
+    def first_from_relay():
+        return pltpu.make_async_remote_copy(
+            src_ref=passing_first,
+            dst_ref=wave.at[0, :, pl.ds(half + q * rows, rows)],
+            send_sem=pass_first_send,
+            recv_sem=first_recv.at[q],
+            device_id=worker(relayed or 0),
+            device_id_type=MESH,
+        )
+
     def send_pieces(i, v):
         here = at_worker(v)
+
+        @pl.when(by_relay(v))
+        def _():
+            for c in range(2):
+                piece_to_relay(i, c).start()
 
         @pl.when(here)
         def _():
@@ -206,7 +275,7 @@
                     ref.at[v, i], volume.at[d * per_slab + i, c, q], vol_recv.at[d * per_slab + i, c, q]
                 ).start()
 
-        @pl.when(jnp.logical_not(here))
+        @pl.when(jnp.logical_not(here | by_relay(v)))
         def _():
             for c in range(2):
                 piece_copy(i, c, v).start()
@@ -233,7 +302,11 @@
                     first.at[v], wave.at[0, :, pl.ds(half + q * rows, rows)], first_recv.at[q]
                 ).start()
 
-            @pl.when(jnp.logical_not(here))
+            @pl.when(by_relay(v))
+            def _():
+                first_to_relay().start()
+
+            @pl.when(jnp.logical_not(here | by_relay(v)))
             def _():
                 first_copy(v).start()
 
@@ -246,6 +319,19 @@
         @pl.loop(0, (per_slab - 1) * views)
         def _(k):
             send_pieces(1 + k // views, k % views)
+
+    @pl.when(passes)
+    def _():
+        @pl.when(d == there)
+        def _():
+            pltpu.make_async_copy(passing_first, passing_first, pass_first_recv).wait()
+            first_from_relay().start()
+
+        @pl.loop(jnp.where(d == there, 1, 0), per_slab)
+        def _(i):
+            for c in range(2):
+                pltpu.make_async_copy(passing.at[i, c], passing.at[i, c], pass_recv.at[i, c]).wait()
+                piece_from_relay(i, c).start()
 
     @pl.when((d > 0) & jnp.logical_not(works))
     def _():
@@ -444,6 +530,17 @@
         def _():
             for c in range(2):
                 piece_copy(i, c, v).wait_send()
+
+    @pl.when(passes)
+    def _():
+        @pl.when(d == there)
+        def _():
+            first_from_relay().wait_send()
+
+        @pl.loop(jnp.where(d == there, 1, 0), per_slab)
+        def _(i):
+            for c in range(2):
+                piece_from_relay(i, c).wait_send()
 
     for v in range(views):
         ref = out_ref.at[:, v, 0]
@@ -516,6 +613,12 @@
             dma((depths, PAIR)),
             dma((views,)),
             pltpu.SemaphoreType.REGULAR((views,)),
+            pltpu.VMEM((per_slab, 2, rows, cols), f32),
+            pltpu.VMEM((2, rows, cols), f32),
+            dma((per_slab, 2)),
+            dma((per_slab, 2)),
+            dma,
+            dma,
         ],
         compiler_params=pltpu.CompilerParams(
             collective_id=0, has_side_effects=True, vmem_limit_bytes=63 * 1024 * 1024

time: 49.6 us -> 51.6 us (1.040)
  the two profiles are of different devices: /device:TPU:0 before, /device:TPU:7 now
where the time goes in v8:
time: 51.6 us; the launch traced here: 51.4 us
  Pallas kernels  51.4 us (100%)
    pallas_call x1, Pallas kernels, per_device(): pl.pallas_call(functools.partial(body, depths, tiles, views, rows, cols,...  49.6 us
    pallas_call x1, Pallas kernels, per_device(): pl.pallas_call(functools.partial(in_order, views), out_shape=shape, in_sp...  1.78 us

profile of v8, /device:TPU:7, one launch (start us, length us, event | category | flops | bytes accessed | tf_op | source)
XLA Modules:
  0.0 51.4 jit_solution(12441850624622247093)
XLA Ops:
  0.0 49.6 %views_by_worker.1.value_ref = f32[2,3,1,32,512]{4,3,2,1,0:T(8,128)} custom-call(f32[2,3,32,512]{3,2,1,0:T(8,128)} %incident_ref.1, f32[3,2,32,512]{3,2,1,0:T(8,128)} %delta_ref.1, f32[3,2,32,512]{3,2,1,0:T(8,128)} %beta_ref.1, bf16[256,256]{1,0:T(8,128)(2,1)} %constant.4.clone.rmat_ref, bf16[2,512,256]{2,1,0:T(8,128)(2,1)} %constant.5.clone.cmat_ref), custom_call_target="tpu_custom_call" | custom-call | tf_op jit(solution)/shard_map/views_by_worker/pallas_call | solution.py:592
  49.7 1.8 %stored_order.1 = f32[2,3,1,32,512]{4,3,2,1,0:T(8,128)} custom-call(s32[3]{0:T(128)} %order_ref.1, f32[2,3,1,32,512]{4,3,2,1,0:T(8,128)} %views_by_worker.1.value_ref), custom_call_target="tpu_custom_call" | custom-call | tf_op jit(solution)/shard_map/stored_order/pallas_call | solution.py:628

commit v9 on v7

--- a/solution.py
+++ b/solution.py
@@ -12,7 +12,7 @@
 HALF = 32
 LANES = 128
 PAIR = 2
-GROUP = 1
+GROUP = 2
 STRIP = 8
 MESH = pl.DeviceIdType.MESH
 

time: 49.6 us -> 50.7 us (1.022)
  Pallas kernels: 49.4 us -> 50.6 us
    pallas_call x1, Pallas kernels: 47.6 us -> 48.8 us  [per_device(): pl.pallas_call(functools.partial(body, depths, tiles, views, rows, cols,...]
where the time goes in v9:
time: 50.7 us; the launch traced here: 50.6 us
  Pallas kernels  50.6 us (100%)
    pallas_call x1, Pallas kernels, per_device(): pl.pallas_call(functools.partial(body, depths, tiles, views, rows, cols,...  48.8 us
    pallas_call x1, Pallas kernels, per_device(): pl.pallas_call(functools.partial(in_order, views), out_shape=shape, in_sp...  1.78 us

profile of v9, /device:TPU:0, one launch (start us, length us, event | category | flops | bytes accessed | tf_op | source)
XLA Modules:
  0.0 50.6 jit_solution(11090710542163905784)
XLA Ops:
  0.0 48.8 %views_by_worker.1.value_ref = f32[2,3,1,32,512]{4,3,2,1,0:T(8,128)} custom-call(f32[2,3,32,512]{3,2,1,0:T(8,128)} %incident_ref.1, f32[3,2,32,512]{3,2,1,0:T(8,128)} %delta_ref.1, f32[3,2,32,512]{3,2,1,0:T(8,128)} %beta_ref.1, bf16[256,256]{1,0:T(8,128)(2,1)} %constant.4.clone.rmat_ref, bf16[2,512,256]{2,1,0:T(8,128)(2,1)} %constant.5.clone.cmat_ref), custom_call_target="tpu_custom_call" | custom-call | tf_op jit(solution)/shard_map/views_by_worker/pallas_call | solution.py:495
  48.8 1.8 %stored_order.1 = f32[2,3,1,32,512]{4,3,2,1,0:T(8,128)} custom-call(s32[3]{0:T(128)} %order_ref.1, f32[2,3,1,32,512]{4,3,2,1,0:T(8,128)} %views_by_worker.1.value_ref), custom_call_target="tpu_custom_call" | custom-call | tf_op jit(solution)/shard_map/stored_order/pallas_call | solution.py:525

commit v10 on v7

--- a/solution.py
+++ b/solution.py
@@ -353,10 +353,6 @@
                                 go.at[mine], inc=1, device_id=(dd, pair * PAIR + qq), device_id_type=MESH
                             )
 
-            @pl.when(s < slices - 1)
-            def _():
-                transmission(s + 1)
-
             count = 2 * span
 
             def rows_done(first_block, last_block):
@@ -414,6 +410,12 @@
                     if len(made) < wanted:
                         joined = rows_done(len(made), wanted)
                         made += [joined[:, k : k + LANES] for k in range(0, joined.shape[1], LANES)]
+                if first_block == 0:
+
+                    @pl.when(s < slices - 1)
+                    def _():
+                        transmission(s + 1)
+
                 pieces = [
                     made[k] if 0 <= k < blocks else outside for k in range(first_block - 1, last_block + 1)
                 ]

time: 49.6 us -> 50.7 us (1.022)
  Pallas kernels: 49.4 us -> 50.6 us
    pallas_call x1, Pallas kernels: 47.6 us -> 48.8 us  [per_device(): pl.pallas_call(functools.partial(body, depths, tiles, views, rows, cols,...]
where the time goes in v10:
time: 50.7 us; the launch traced here: 50.6 us
  Pallas kernels  50.6 us (100%)
    pallas_call x1, Pallas kernels, per_device(): pl.pallas_call(functools.partial(body, depths, tiles, views, rows, cols,...  48.8 us
    pallas_call x1, Pallas kernels, per_device(): pl.pallas_call(functools.partial(in_order, views), out_shape=shape, in_sp...  1.78 us

profile of v10, /device:TPU:0, one launch (start us, length us, event | category | flops | bytes accessed | tf_op | source)
XLA Modules:
  0.0 50.6 jit_solution(16418985198536716859)
XLA Ops:
  0.0 48.8 %views_by_worker.1.value_ref = f32[2,3,1,32,512]{4,3,2,1,0:T(8,128)} custom-call(f32[2,3,32,512]{3,2,1,0:T(8,128)} %incident_ref.1, f32[3,2,32,512]{3,2,1,0:T(8,128)} %delta_ref.1, f32[3,2,32,512]{3,2,1,0:T(8,128)} %beta_ref.1, bf16[256,256]{1,0:T(8,128)(2,1)} %constant.4.clone.rmat_ref, bf16[2,512,256]{2,1,0:T(8,128)(2,1)} %constant.5.clone.cmat_ref), custom_call_target="tpu_custom_call" | custom-call | tf_op jit(solution)/shard_map/views_by_worker/pallas_call | solution.py:497
  48.8 1.8 %stored_order.1 = f32[2,3,1,32,512]{4,3,2,1,0:T(8,128)} custom-call(s32[3]{0:T(128)} %order_ref.1, f32[2,3,1,32,512]{4,3,2,1,0:T(8,128)} %views_by_worker.1.value_ref), custom_call_target="tpu_custom_call" | custom-call | tf_op jit(solution)/shard_map/stored_order/pallas_call | solution.py:527

commit v11 on v7

--- a/solution.py
+++ b/solution.py
@@ -410,10 +410,10 @@
             made = []
             for first_block in range(0, blocks, GROUP):
                 last_block = min(first_block + GROUP, blocks)
-                for wanted in (last_block, min(last_block + 1, blocks)):
-                    if len(made) < wanted:
-                        joined = rows_done(len(made), wanted)
-                        made += [joined[:, k : k + LANES] for k in range(0, joined.shape[1], LANES)]
+                wanted = min(last_block + 1, blocks)
+                if len(made) < wanted:
+                    joined = rows_done(len(made), wanted)
+                    made += [joined[:, k : k + LANES] for k in range(0, joined.shape[1], LANES)]
                 pieces = [
                     made[k] if 0 <= k < blocks else outside for k in range(first_block - 1, last_block + 1)
                 ]

time: 49.6 us -> 49.4 us (level)
  no operation moved by 1% of the time
where the time goes in v11:
time: 49.4 us; the launch traced here: 49.2 us
  Pallas kernels  49.2 us (100%)
    pallas_call x1, Pallas kernels, per_device(): pl.pallas_call(functools.partial(body, depths, tiles, views, rows, cols,...  47.5 us
    pallas_call x1, Pallas kernels, per_device(): pl.pallas_call(functools.partial(in_order, views), out_shape=shape, in_sp...  1.78 us

profile of v11, /device:TPU:0, one launch (start us, length us, event | category | flops | bytes accessed | tf_op | source)
XLA Modules:
  0.0 49.2 jit_solution(15149157242175486849)
XLA Ops:
  0.0 47.5 %views_by_worker.1.value_ref = f32[2,3,1,32,512]{4,3,2,1,0:T(8,128)} custom-call(f32[2,3,32,512]{3,2,1,0:T(8,128)} %incident_ref.1, f32[3,2,32,512]{3,2,1,0:T(8,128)} %delta_ref.1, f32[3,2,32,512]{3,2,1,0:T(8,128)} %beta_ref.1, bf16[256,256]{1,0:T(8,128)(2,1)} %constant.4.clone.rmat_ref, bf16[2,512,256]{2,1,0:T(8,128)(2,1)} %constant.5.clone.cmat_ref), custom_call_target="tpu_custom_call" | custom-call | tf_op jit(solution)/shard_map/views_by_worker/pallas_call | solution.py:495
  47.5 1.8 %stored_order.1 = f32[2,3,1,32,512]{4,3,2,1,0:T(8,128)} custom-call(s32[3]{0:T(128)} %order_ref.1, f32[2,3,1,32,512]{4,3,2,1,0:T(8,128)} %views_by_worker.1.value_ref), custom_call_target="tpu_custom_call" | custom-call | tf_op jit(solution)/shard_map/stored_order/pallas_call | solution.py:525
